TPU v7x, 128 devices: a whole 4x4x4 slice. The times are simulated.
128 devices in a mesh: slab: 8 (over y_lo, z), energy: 16 (over x, y_hi, core).
Axes of the slice: x: 4, y: 4 (y_hi: 2, y_lo: 2; y = y_hi * 2 + y_lo), z: 4, core: 2. Of those that a mesh axis runs over, the one named last changes fastest.
Arguments:
- green_ret: bfloat16 [8, 16, 2, 1536, 1536], P('slab', 'energy'), may hold values from -2.5 to 2.5
- prev_lesser: float32 [8, 16, 2, 1536, 128], P('slab', 'energy'), may hold values from -8 to 8
- coupling_index: int32 [8, 3, 2], P('slab'), may hold values from 0 to 1, as said below
- coupling_values: float32 [8, 3, 128, 128], P('slab'), may hold values from -1.5 to 1.5
- phonon_shift: int32 [3], replicated, may hold values from 1 to 8, as said below
- phonon_weight: float32 [2, 3], replicated, may hold values from 0.1 to 0.5
Outputs:
- retarded_blocks: float32 [8, 16, 2, 1536, 128], P('slab', 'energy')
- lesser_blocks: float32 [8, 16, 2, 1536, 128], P('slab', 'energy')
Inputs may be any that keep to these rules, and one draw needn't show every extreme that they name: `coupling_index`: within one slab the 3 block positions are distinct: each of the 2 diagonal blocks once and one block off the diagonal, in drawn order. `phonon_shift`: the 3 shifts are distinct; one of them is 1 and one is 8.
All inputs are finite; a program needn't handle non-finite values.
Results may differ from a plain program's by a relative error of at most 0.0052.
Values sent between devices are 32-bit elements; how exact they have to be, the bound alone decides.
A program may use at most 192 MiB of HBM per device.

v0:
```python
import jax
import jax.numpy as jnp
from jax import lax
from jax.sharding import PartitionSpec as P

SLAB_ORBITALS = 1536
BW = 256
BLK = 128
NBLK = 12
NBW = 2


FULL_PRECISION = lax.Precision.HIGHEST


def passed_along(value, axis, steps):
    count = lax.axis_size(axis)
    leading, last = (max(0, -steps), min(count, count - steps))
    return lax.ppermute(value, axis, [(source, source + steps) for source in range(leading, last)])


def product(pattern, left_factor, right_factor, precise):
    if precise:
        return jnp.einsum(
            pattern,
            left_factor,
            right_factor,
            precision=FULL_PRECISION,
            preferred_element_type=jnp.float32,
        )
    return jnp.einsum(pattern, left_factor, right_factor, preferred_element_type=jnp.float32)


def complex_product(pattern, left_factor, right_factor, precise):
    real_part = product(pattern, left_factor[0], right_factor[0], precise) - product(
        pattern, left_factor[1], right_factor[1], precise
    )
    imag_part = product(pattern, left_factor[0], right_factor[1], precise) + product(
        pattern, left_factor[1], right_factor[0], precise
    )
    return jnp.stack([real_part, imag_part])


def conjugate_product(pattern, left_factor, right_factor, precise):
    real_part = product(pattern, left_factor[0], right_factor[0], precise) + product(
        pattern, left_factor[1], right_factor[1], precise
    )
    imag_part = product(pattern, left_factor[1], right_factor[0], precise) - product(
        pattern, left_factor[0], right_factor[1], precise
    )
    return jnp.stack([real_part, imag_part])


def adjoint(matrix):
    return jnp.stack([matrix[0].T, -matrix[1].T])


def block_adjoint(blocks):
    shaped = jnp.swapaxes(blocks.reshape(2, NBLK, BLK, BLK), 2, 3)
    return jnp.stack([shaped[0], -shaped[1]]).reshape(2, SLAB_ORBITALS, BLK)


def blocks_product(left_factor, right_factor):
    inner_size = left_factor.shape[-1]
    return complex_product(
        "nak,knb->nab",
        left_factor.reshape(2, NBLK, BLK, inner_size),
        right_factor.reshape(2, inner_size, NBLK, BLK),
        False,
    ).reshape(2, SLAB_ORBITALS, BLK)


def blocks_adjoint_product(left_factor, right_factor):
    inner_size = left_factor.shape[-1]
    return conjugate_product(
        "nak,nbk->nab",
        left_factor.reshape(2, NBLK, BLK, inner_size),
        right_factor.reshape(2, NBLK, BLK, inner_size),
        False,
    ).reshape(2, SLAB_ORBITALS, BLK)


def diagonal_blocks(green_fn):
    shaped = green_fn.reshape(2, NBLK, BLK, NBLK, BLK)
    return jnp.einsum("pnanb->pnab", shaped).astype(jnp.float32).reshape(2, SLAB_ORBITALS, BLK)


def dense_coupling(block_index, block_values):
    positions = jnp.arange(NBW, dtype=jnp.int32)[None, :]
    row_select = (block_index[:, 0:1] == positions).astype(jnp.float32)
    column_select = (block_index[:, 1:2] == positions).astype(jnp.float32)
    dense = jnp.einsum(
        "br,bc,bij->ricj", row_select, column_select, block_values, precision=FULL_PRECISION
    )
    return dense.reshape(BW, BW)


def partner_weights(targets, sources, phonon_shift, phonon_weight):
    target_column = jnp.asarray(targets)[..., None]
    source_column = jnp.asarray(sources)[..., None]
    emission = jnp.where(source_column == target_column + phonon_shift, phonon_weight[0], 0.0)
    absorption = jnp.where(source_column == target_column - phonon_shift, phonon_weight[1], 0.0)
    return jnp.sum(emission + absorption, axis=-1)


def sandwich_left(coupling, matrix):
    return jnp.einsum("ki,pkl,lj->pij", coupling, matrix, coupling, precision=FULL_PRECISION)


def sandwich_right(coupling, matrix):
    return jnp.einsum("ik,pkl,jl->pij", coupling, matrix, coupling, precision=FULL_PRECISION)


def local_terms(green_fn, self_energy):
    sigma_rounded = self_energy.astype(jnp.bfloat16).reshape(2, NBLK, BLK, BLK)
    scaled = complex_product(
        "ank,nkl->anl", green_fn.reshape(2, SLAB_ORBITALS, NBLK, BLK), sigma_rounded, False
    )
    scaled = scaled.reshape(2, SLAB_ORBITALS, SLAB_ORBITALS).astype(jnp.bfloat16)
    outer_right = conjugate_product("ik,jk->ij", scaled[:, SLAB_ORBITALS - BW :], green_fn, False)
    outer_left = conjugate_product("ik,jk->ij", scaled[:, :BW], green_fn[:, :BW], False)
    outer_blocks = blocks_adjoint_product(scaled, green_fn)
    return (outer_right, outer_left, outer_blocks)


def body(green_ret, prev_lesser, coupling_index, coupling_values, phonon_shift, phonon_weight):
    green_fn = green_ret[0, 0]
    coupling = dense_coupling(coupling_index[0], coupling_values[0])
    my_energy = lax.axis_index("energy")
    received_piece = lax.all_gather(prev_lesser, "energy", axis=1, tiled=True)
    sources = jnp.arange(received_piece.shape[1], dtype=jnp.int32)
    weights = partner_weights(my_energy, sources, phonon_shift, phonon_weight)
    self_energy = jnp.einsum("c,cpak->pak", weights, received_piece[0], precision=FULL_PRECISION)
    outer_right, outer_left, outer_blocks = local_terms(green_fn, self_energy)
    corner = green_fn[:, SLAB_ORBITALS - BW :, :BW].astype(jnp.float32)
    transfer = jnp.einsum("ki,pkj->pij", coupling, corner, precision=FULL_PRECISION)
    source = sandwich_left(coupling, outer_right[:, :, SLAB_ORBITALS - BW :])

    def advance(boundary_state):
        return (
            conjugate_product(
                "ik,jk->ij",
                complex_product("ik,kj->ij", transfer, boundary_state, True),
                transfer,
                True,
            )
            + source
        )

    slab_count = lax.axis_size("slab")
    my_slab = lax.axis_index("slab")

    def forward_turn(step_index, carried):
        received = passed_along(carried[1], "slab", 1)
        updated = lax.cond(
            step_index + 1 == my_slab,
            lambda operands: advance(operands[0]),
            lambda operands: operands[1],
            (received, carried[1]),
        )
        return (received, updated)

    boundary_state, _ = lax.fori_loop(
        0, slab_count - 1, forward_turn, (jnp.zeros_like(source), source)
    )
    left_columns = green_fn[:, :, :BW]
    coupled = complex_product(
        "ik,kj->ij", left_columns, boundary_state.astype(jnp.bfloat16), False
    ).astype(jnp.bfloat16)
    far_right = outer_right + conjugate_product(
        "ik,jk->ij", coupled[:, SLAB_ORBITALS - BW :], left_columns, False
    )
    left_block = outer_left + conjugate_product(
        "ik,jk->ij", coupled[:, :BW], green_fn[:, :BW, :BW], False
    )
    lesser_local = outer_blocks + blocks_adjoint_product(coupled, left_columns)
    upper_corner = green_fn[:, :BW, SLAB_ORBITALS - BW :].astype(jnp.float32)
    inward = jnp.einsum("pik,kj->pij", upper_corner, coupling, precision=FULL_PRECISION)
    outward = jnp.einsum("ki,pkj->pij", coupling, far_right[:, :, :BW], precision=FULL_PRECISION)
    diagonal_corner = green_fn[:, :BW, :BW].astype(jnp.float32)

    def retreat(corner_pair):
        through = complex_product("ik,kj->ij", inward, corner_pair[0], True)
        mixed_term = complex_product("ik,kj->ij", through, outward, True)
        retarded_corner = diagonal_corner + complex_product("ik,kj->ij", through, transfer, True)
        lesser_corner = (
            left_block
            + mixed_term
            + adjoint(mixed_term)
            + conjugate_product(
                "ik,jk->ij",
                complex_product("ik,kj->ij", inward, corner_pair[1], True),
                inward,
                True,
            )
        )
        return jnp.stack([retarded_corner, lesser_corner])

    initial_pair = jnp.stack([diagonal_corner, left_block])

    def backward_turn(step_index, carried):
        received = passed_along(carried[1], "slab", -1)
        updated = lax.cond(
            slab_count - 2 - step_index == my_slab,
            lambda operands: retreat(operands[0]),
            lambda operands: operands[1],
            (received, carried[1]),
        )
        return (received, updated)

    incoming, _ = lax.fori_loop(
        0, slab_count - 1, backward_turn, (jnp.zeros_like(initial_pair), initial_pair)
    )
    retarded_in = incoming[0]
    lesser_in = incoming[1]
    retarded_far = sandwich_right(coupling, retarded_in)
    lesser_far = sandwich_right(coupling, lesser_in)
    right_columns = green_fn[:, :, SLAB_ORBITALS - BW :]
    retarded_weighted = complex_product(
        "ik,kj->ij", right_columns, retarded_far.astype(jnp.bfloat16), False
    ).astype(jnp.bfloat16)
    lesser_weighted = complex_product(
        "ik,kj->ij", right_columns, lesser_far.astype(jnp.bfloat16), False
    ).astype(jnp.bfloat16)
    retarded = diagonal_blocks(green_fn) + blocks_product(
        retarded_weighted, green_fn[:, SLAB_ORBITALS - BW :, :]
    )
    mixed_blocks = blocks_product(retarded_weighted, far_right.astype(jnp.bfloat16))
    lesser = (
        lesser_local
        + mixed_blocks
        + block_adjoint(mixed_blocks)
        + blocks_adjoint_product(lesser_weighted, right_columns)
    )
    return (retarded[None, None], lesser[None, None])


def solution(mesh):
    placed = (
        P("slab", "energy", None, None, None),
        P("slab", "energy", None, None, None),
        P("slab", None, None),
        P("slab", None, None, None),
        P(),
        P(),
    )
    return jax.shard_map(
        body,
        mesh=mesh,
        in_specs=placed,
        out_specs=(P("slab", "energy", None, None, None), P("slab", "energy", None, None, None)),
        check_vma=False,
    )
```

profile of v0, /device:TPU:0, one launch (start us, length us, event | category | flops | bytes accessed | tf_op | source)
XLA Modules:
  0.0 817.4 jit_solution(7374198031576881465)
XLA Ops:
  7.9 17.9 %reshape_squeeze.2 = bf16[2,12,128,12,128]{4,3,2,1,0:T(8,128)(2,1)} reshape(bf16[1,1,2,1536,1536]{4,3,2,1,0:T(8,128)(2,1)} %param.14) | data formatting | bytes 18874368 | tf_op jit(solution)/shard_map/reshape;squeeze | solution.py:84
  71.0 90.9 %all-gather.2.cloned.1.call-done = f32[1,16,2,1536,128]{4,3,2,0,1:T(8,128)} async-done(((f32[1,1,2,1536,128]{4,3,2,0,1:T(8,128)}), f32[1,16,2,1536,128]{4,3,2,0,1:T(8,128)}) %all-gather.2.cloned.1.call-update) | async-done | bytes 25165840 | tf_op jit(solution)/shard_map/all_gather | solution.py:130
  161.8 40.3 %fusion.103 = f32[1,2,1536,128]{3,0,2,1:T(1,128)S(1)} fusion(f32[16,2,1536,128]{3,2,1,0:T(8,128)} %bitcast.509, f32[16]{0:T(128)S(1)} %add_reduce_fusion), kind=kOutput, calls=%fused_computation.123 | convolution fusion | flops 75497472 | bytes 26738752 | tf_op jit(solution)/shard_map/c,cpak->pak/dot_general | solution.py:133
  234.8 112.3 %while.36 = (s32[]{:T(128)}, f32[2,256,256]{2,1,0:T(8,128)}, f32[2,256,256]{2,1,0:T(8,128)S(1)}, s32[]{:T(128)}, f32[2,256,256]{2,1,0:T(8,128)S(1)}, /*index=5*/f32[2,256,256]{2,1,0:T(8,128)S(1)}, s32[]{:T(128)}) while((s32[]{:T(128)}, f32[2,256,256]{2,1,0:T(8,128)}, f32[2,256,256]{2,1,0:T(8,128)S(1)}, s32[]{:T(128)}, ...), condition=%wide.region_5.6_spmd, body=%wide.region_2.5_spmd.sunk | while | flops 1611137024 | bytes 11010211 | solution.py:163
  239.2 10.8 %collective-permute-done = f32[2,256,256]{2,1,0:T(8,128)} collective-permute-done((f32[2,256,256]{2,1,0:T(8,128)S(1)}, f32[2,256,256]{2,1,0:T(8,128)}, u32[]{:S(2)}, u32[]{:S(2)}) %collective-permute-start) | collective-permute-done | bytes 524320 | tf_op jit(solution)/shard_map/while/body/eval_jaxpr/ppermute | solution.py:19
  249.9 12.4 %collective-permute-start = (f32[2,256,256]{2,1,0:T(8,128)S(1)}, f32[2,256,256]{2,1,0:T(8,128)}, u32[]{:S(2)}, u32[]{:S(2)}) collective-permute-start(f32[2,256,256]{2,1,0:T(8,128)S(1)} %get-tuple-element.500), channel_id=1, source_target_pairs={{0,16},{16,32},{32,48},{48,64},{64,80},{80,96},{96,112},{1,17},{17... | collective-permute-start | bytes 1572872 | tf_op jit(solution)/shard_map/while/body/eval_jaxpr/ppermute | solution.py:19
  262.4 10.0 %collective-permute-done = f32[2,256,256]{2,1,0:T(8,128)} collective-permute-done((f32[2,256,256]{2,1,0:T(8,128)S(1)}, f32[2,256,256]{2,1,0:T(8,128)}, u32[]{:S(2)}, u32[]{:S(2)}) %collective-permute-start) | collective-permute-done | bytes 524320 | tf_op jit(solution)/shard_map/while/body/eval_jaxpr/ppermute | solution.py:19
  277.6 9.0 %collective-permute-done = f32[2,256,256]{2,1,0:T(8,128)} collective-permute-done((f32[2,256,256]{2,1,0:T(8,128)S(1)}, f32[2,256,256]{2,1,0:T(8,128)}, u32[]{:S(2)}, u32[]{:S(2)}) %collective-permute-start) | collective-permute-done | bytes 524320 | tf_op jit(solution)/shard_map/while/body/eval_jaxpr/ppermute | solution.py:19
  286.7 10.5 %collective-permute-start = (f32[2,256,256]{2,1,0:T(8,128)S(1)}, f32[2,256,256]{2,1,0:T(8,128)}, u32[]{:S(2)}, u32[]{:S(2)}) collective-permute-start(f32[2,256,256]{2,1,0:T(8,128)S(1)} %get-tuple-element.500), channel_id=1, source_target_pairs={{0,16},{16,32},{32,48},{48,64},{64,80},{80,96},{96,112},{1,17},{17... | collective-permute-start | bytes 1572872 | tf_op jit(solution)/shard_map/while/body/eval_jaxpr/ppermute | solution.py:19
  297.1 8.4 %collective-permute-done = f32[2,256,256]{2,1,0:T(8,128)} collective-permute-done((f32[2,256,256]{2,1,0:T(8,128)S(1)}, f32[2,256,256]{2,1,0:T(8,128)}, u32[]{:S(2)}, u32[]{:S(2)}) %collective-permute-start) | collective-permute-done | bytes 524320 | tf_op jit(solution)/shard_map/while/body/eval_jaxpr/ppermute | solution.py:19
  318.3 10.7 %collective-permute-start = (f32[2,256,256]{2,1,0:T(8,128)S(1)}, f32[2,256,256]{2,1,0:T(8,128)}, u32[]{:S(2)}, u32[]{:S(2)}) collective-permute-start(f32[2,256,256]{2,1,0:T(8,128)S(1)} %get-tuple-element.500), channel_id=1, source_target_pairs={{0,16},{16,32},{32,48},{48,64},{64,80},{80,96},{96,112},{1,17},{17... | collective-permute-start | bytes 1572872 | tf_op jit(solution)/shard_map/while/body/eval_jaxpr/ppermute | solution.py:19
  384.3 321.1 %while.37 = (s32[]{:T(128)}, f32[2,2,256,256]{3,2,1,0:T(8,128)}, f32[2,2,256,256]{3,2,1,0:T(8,128)}, s32[]{:T(128)}, f32[2,256,256]{2,1,0:T(8,128)S(1)}, /*index...) while((s32[]{:T(128)}, f32[2,2,256,256]{3,2,1,0:T(8,128)}, ...), condition=%wide.region_9.10_spmd, body=%wide.region_6.9_spmd.sunk | while | flops 4028563456 | bytes 33554688 | solution.py:211
  385.8 29.4 %collective-permute-done.1 = f32[2,2,256,256]{3,2,1,0:T(8,128)} collective-permute-done((f32[2,2,256,256]{3,2,1,0:T(8,128)}, f32[2,2,256,256]{3,2,1,0:T(8,128)}, u32[]{:S(2)}, u32[]{:S(2)}) %collective-permute-start.1) | collective-permute-done | bytes 1048608 | tf_op jit(solution)/shard_map/while/body/eval_jaxpr/ppermute | solution.py:19
  416.4 23.1 %collective-permute-done.1 = f32[2,2,256,256]{3,2,1,0:T(8,128)} collective-permute-done((f32[2,2,256,256]{3,2,1,0:T(8,128)}, f32[2,2,256,256]{3,2,1,0:T(8,128)}, u32[]{:S(2)}, u32[]{:S(2)}) %collective-permute-start.1) | collective-permute-done | bytes 1048608 | tf_op jit(solution)/shard_map/while/body/eval_jaxpr/ppermute | solution.py:19
  440.8 24.5 %collective-permute-done.1 = f32[2,2,256,256]{3,2,1,0:T(8,128)} collective-permute-done((f32[2,2,256,256]{3,2,1,0:T(8,128)}, f32[2,2,256,256]{3,2,1,0:T(8,128)}, u32[]{:S(2)}, u32[]{:S(2)}) %collective-permute-start.1) | collective-permute-done | bytes 1048608 | tf_op jit(solution)/shard_map/while/body/eval_jaxpr/ppermute | solution.py:19
  466.5 22.0 %collective-permute-done.1 = f32[2,2,256,256]{3,2,1,0:T(8,128)} collective-permute-done((f32[2,2,256,256]{3,2,1,0:T(8,128)}, f32[2,2,256,256]{3,2,1,0:T(8,128)}, u32[]{:S(2)}, u32[]{:S(2)}) %collective-permute-start.1) | collective-permute-done | bytes 1048608 | tf_op jit(solution)/shard_map/while/body/eval_jaxpr/ppermute | solution.py:19
  489.9 23.7 %collective-permute-done.1 = f32[2,2,256,256]{3,2,1,0:T(8,128)} collective-permute-done((f32[2,2,256,256]{3,2,1,0:T(8,128)}, f32[2,2,256,256]{3,2,1,0:T(8,128)}, u32[]{:S(2)}, u32[]{:S(2)}) %collective-permute-start.1) | collective-permute-done | bytes 1048608 | tf_op jit(solution)/shard_map/while/body/eval_jaxpr/ppermute | solution.py:19
  514.9 21.2 %collective-permute-done.1 = f32[2,2,256,256]{3,2,1,0:T(8,128)} collective-permute-done((f32[2,2,256,256]{3,2,1,0:T(8,128)}, f32[2,2,256,256]{3,2,1,0:T(8,128)}, u32[]{:S(2)}, u32[]{:S(2)}) %collective-permute-start.1) | collective-permute-done | bytes 1048608 | tf_op jit(solution)/shard_map/while/body/eval_jaxpr/ppermute | solution.py:19
  537.3 147.1 %collective-permute-done.1 = f32[2,2,256,256]{3,2,1,0:T(8,128)} collective-permute-done((f32[2,2,256,256]{3,2,1,0:T(8,128)}, f32[2,2,256,256]{3,2,1,0:T(8,128)}, u32[]{:S(2)}, u32[]{:S(2)}) %collective-permute-start.1) | collective-permute-done | bytes 1048608 | tf_op jit(solution)/shard_map/while/body/eval_jaxpr/ppermute | solution.py:19
  684.4 20.8 %conditional.5 = (f32[2,2,256,256]{3,2,1,0:T(8,128)}) conditional(s32[]{:T(128)} %convert_element_type.60, f32[2,2,256,256]{3,2,1,0:T(8,128)} %get-tuple-element.525, (f32[2,256,256]{2,1,0:T(8,128)S(1)}, f32[2,2,256,256]{3,2,1,0:T(8,128)}, f32[2,256,256]{2,1,0:T(8,128)S(1)}, f32[2,256,256]{2,1,0:T(8,128)}, f32[2,256,256]{2,1,0:T(8,128)S(1)}, ...), branch_computations={%region_7.7_spmd, %region_8.8_spmd} | conditional | flops 4028563456 | bytes 29360164 | solution.py:203
  755.6 9.4 %reshape.392 = bf16[12,128,1536]{1,0,2:T(8,128)(2,1)} reshape(bf16[1536,12,128]{0,2,1:T(8,128)(2,1)} %bitcast.522) | data formatting | bytes 9437184 | tf_op jit(solution)/shard_map/squeeze | solution.py:45
  765.0 8.7 %copy.272 = bf16[12,128,1536]{2,1,0:T(8,128)(2,1)} copy(bf16[12,128,1536]{1,0,2:T(8,128)(2,1)} %reshape.392) | data formatting | bytes 9437184 | tf_op jit(solution)/shard_map/squeeze | solution.py:45
  773.7 9.4 %reshape.393 = bf16[12,128,1536]{1,0,2:T(8,128)(2,1)} reshape(bf16[1536,12,128]{0,2,1:T(8,128)(2,1)} %bitcast.527) | data formatting | bytes 9437184 | tf_op jit(solution)/shard_map/squeeze | solution.py:46
  783.2 8.7 %copy.273 = bf16[12,128,1536]{2,1,0:T(8,128)(2,1)} copy(bf16[12,128,1536]{1,0,2:T(8,128)(2,1)} %reshape.393) | data formatting | bytes 9437184 | tf_op jit(solution)/shard_map/squeeze | solution.py:46
  (265 shorter events, 253.4 us)
Async XLA Ops:
  7.2 154.7 %all-gather.2.cloned.1.call-start = ((), (), s32[]{:S(2)}) async-start(), calls=%async_computation | async-start | bytes 26738688 | tf_op jit(solution)/shard_map/all_gather | solution.py:130
  161.8 40.5 %slice-start.3 = ((s8[4718592]{0:T(1024)(128)(4,1)}), s8[4194304]{0:T(1024)(128)(4,1)S(1)}, s32[]{:S(2)}) async-start(s8[4718592]{0:T(1024)(128)(4,1)} %bitcast.490), calls=%async_computation.4 | async-start | bytes 8388608
  161.8 40.5 %slice-start.4 = ((s8[4718592]{0:T(1024)(128)(4,1)}), s8[524288]{0:T(1024)(128)(4,1)S(1)}, s32[]{:S(2)}) async-start(s8[4718592]{0:T(1024)(128)(4,1)} %bitcast.490), calls=%async_computation.5 | async-start | bytes 1048576
  207.4 9.5 %slice-start = ((s8[9437184]{0:T(1024)(128)(4,1)}), s8[4194304]{0:T(1024)(128)(4,1)S(1)}, s32[]{:S(2)}) async-start(s8[9437184]{0:T(1024)(128)(4,1)} %bitcast.488), calls=%async_computation.1 | async-start | bytes 8388608
  207.4 9.5 %slice-start.1 = ((s8[9437184]{0:T(1024)(128)(4,1)}), s8[4194304]{0:T(1024)(128)(4,1)S(1)}, s32[]{:S(2)}) async-start(s8[9437184]{0:T(1024)(128)(4,1)} %bitcast.488), calls=%async_computation.2 | async-start | bytes 8388608
  208.9 8.0 slice-start.2
  234.9 15.1 %collective-permute-start = (f32[2,256,256]{2,1,0:T(8,128)S(1)}, f32[2,256,256]{2,1,0:T(8,128)}, u32[]{:S(2)}, u32[]{:S(2)}) collective-permute-start(f32[2,256,256]{2,1,0:T(8,128)S(1)} %get-tuple-element.500), channel_id=1, source_target_pairs={{0,16},{16,32},{32,48},{48,64},{64,80},{80,96},{96,112},{1,17},{17... | collective-permute-start | bytes 1572872 | tf_op jit(solution)/shard_map/while/body/eval_jaxpr/ppermute | solution.py:19
  249.9 22.4 %collective-permute-start = (f32[2,256,256]{2,1,0:T(8,128)S(1)}, f32[2,256,256]{2,1,0:T(8,128)}, u32[]{:S(2)}, u32[]{:S(2)}) collective-permute-start(f32[2,256,256]{2,1,0:T(8,128)S(1)} %get-tuple-element.500), channel_id=1, source_target_pairs={{0,16},{16,32},{32,48},{48,64},{64,80},{80,96},{96,112},{1,17},{17... | collective-permute-start | bytes 1572872 | tf_op jit(solution)/shard_map/while/body/eval_jaxpr/ppermute | solution.py:19
  272.3 14.3 %collective-permute-start = (f32[2,256,256]{2,1,0:T(8,128)S(1)}, f32[2,256,256]{2,1,0:T(8,128)}, u32[]{:S(2)}, u32[]{:S(2)}) collective-permute-start(f32[2,256,256]{2,1,0:T(8,128)S(1)} %get-tuple-element.500), channel_id=1, source_target_pairs={{0,16},{16,32},{32,48},{48,64},{64,80},{80,96},{96,112},{1,17},{17... | collective-permute-start | bytes 1572872 | tf_op jit(solution)/shard_map/while/body/eval_jaxpr/ppermute | solution.py:19
  286.7 18.9 %collective-permute-start = (f32[2,256,256]{2,1,0:T(8,128)S(1)}, f32[2,256,256]{2,1,0:T(8,128)}, u32[]{:S(2)}, u32[]{:S(2)}) collective-permute-start(f32[2,256,256]{2,1,0:T(8,128)S(1)} %get-tuple-element.500), channel_id=1, source_target_pairs={{0,16},{16,32},{32,48},{48,64},{64,80},{80,96},{96,112},{1,17},{17... | collective-permute-start | bytes 1572872 | tf_op jit(solution)/shard_map/while/body/eval_jaxpr/ppermute | solution.py:19
  305.5 12.8 %collective-permute-start = (f32[2,256,256]{2,1,0:T(8,128)S(1)}, f32[2,256,256]{2,1,0:T(8,128)}, u32[]{:S(2)}, u32[]{:S(2)}) collective-permute-start(f32[2,256,256]{2,1,0:T(8,128)S(1)} %get-tuple-element.500), channel_id=1, source_target_pairs={{0,16},{16,32},{32,48},{48,64},{64,80},{80,96},{96,112},{1,17},{17... | collective-permute-start | bytes 1572872 | tf_op jit(solution)/shard_map/while/body/eval_jaxpr/ppermute | solution.py:19
  318.3 17.6 %collective-permute-start = (f32[2,256,256]{2,1,0:T(8,128)S(1)}, f32[2,256,256]{2,1,0:T(8,128)}, u32[]{:S(2)}, u32[]{:S(2)}) collective-permute-start(f32[2,256,256]{2,1,0:T(8,128)S(1)} %get-tuple-element.500), channel_id=1, source_target_pairs={{0,16},{16,32},{32,48},{48,64},{64,80},{80,96},{96,112},{1,17},{17... | collective-permute-start | bytes 1572872 | tf_op jit(solution)/shard_map/while/body/eval_jaxpr/ppermute | solution.py:19
  335.9 11.2 %collective-permute-start = (f32[2,256,256]{2,1,0:T(8,128)S(1)}, f32[2,256,256]{2,1,0:T(8,128)}, u32[]{:S(2)}, u32[]{:S(2)}) collective-permute-start(f32[2,256,256]{2,1,0:T(8,128)S(1)} %get-tuple-element.500), channel_id=1, source_target_pairs={{0,16},{16,32},{32,48},{48,64},{64,80},{80,96},{96,112},{1,17},{17... | collective-permute-start | bytes 1572872 | tf_op jit(solution)/shard_map/while/body/eval_jaxpr/ppermute | solution.py:19
  356.5 9.5 %copy-start.21 = (bf16[256,1536]{1,0:T(8,128)(2,1)}, bf16[256,1536]{1,0:T(8,128)(2,1)S(1)}, u32[]{:S(2)}) copy-start(bf16[256,1536]{1,0:T(8,128)(2,1)S(1)} %fusion.128) | copy-start | bytes 2359300
  360.9 10.0 %copy-start.22 = (bf16[256,1536]{1,0:T(8,128)(2,1)}, bf16[256,1536]{1,0:T(8,128)(2,1)S(1)}, u32[]{:S(2)}) copy-start(bf16[256,1536]{1,0:T(8,128)(2,1)S(1)} %fusion.129) | copy-start | bytes 2359300
  384.5 30.7 %collective-permute-start.1 = (f32[2,2,256,256]{3,2,1,0:T(8,128)}, f32[2,2,256,256]{3,2,1,0:T(8,128)}, u32[]{:S(2)}, u32[]{:S(2)}) collective-permute-start(f32[2,2,256,256]{3,2,1,0:T(8,128)} %get-tuple-element.525), channel_id=1, source_target_pairs={{16,0},{32,16},{48,32},{64,48},{80,64},{96,80},{112,96},{17,1},{33... | collective-permute-start | bytes 3145736 | tf_op jit(solution)/shard_map/while/body/eval_jaxpr/ppermute | solution.py:19
  415.1 24.4 %collective-permute-start.1 = (f32[2,2,256,256]{3,2,1,0:T(8,128)}, f32[2,2,256,256]{3,2,1,0:T(8,128)}, u32[]{:S(2)}, u32[]{:S(2)}) collective-permute-start(f32[2,2,256,256]{3,2,1,0:T(8,128)} %get-tuple-element.525), channel_id=1, source_target_pairs={{16,0},{32,16},{48,32},{64,48},{80,64},{96,80},{112,96},{17,1},{33... | collective-permute-start | bytes 3145736 | tf_op jit(solution)/shard_map/while/body/eval_jaxpr/ppermute | solution.py:19
  439.5 25.7 %collective-permute-start.1 = (f32[2,2,256,256]{3,2,1,0:T(8,128)}, f32[2,2,256,256]{3,2,1,0:T(8,128)}, u32[]{:S(2)}, u32[]{:S(2)}) collective-permute-start(f32[2,2,256,256]{3,2,1,0:T(8,128)} %get-tuple-element.525), channel_id=1, source_target_pairs={{16,0},{32,16},{48,32},{64,48},{80,64},{96,80},{112,96},{17,1},{33... | collective-permute-start | bytes 3145736 | tf_op jit(solution)/shard_map/while/body/eval_jaxpr/ppermute | solution.py:19
  465.2 23.3 %collective-permute-start.1 = (f32[2,2,256,256]{3,2,1,0:T(8,128)}, f32[2,2,256,256]{3,2,1,0:T(8,128)}, u32[]{:S(2)}, u32[]{:S(2)}) collective-permute-start(f32[2,2,256,256]{3,2,1,0:T(8,128)} %get-tuple-element.525), channel_id=1, source_target_pairs={{16,0},{32,16},{48,32},{64,48},{80,64},{96,80},{112,96},{17,1},{33... | collective-permute-start | bytes 3145736 | tf_op jit(solution)/shard_map/while/body/eval_jaxpr/ppermute | solution.py:19
  488.6 25.0 %collective-permute-start.1 = (f32[2,2,256,256]{3,2,1,0:T(8,128)}, f32[2,2,256,256]{3,2,1,0:T(8,128)}, u32[]{:S(2)}, u32[]{:S(2)}) collective-permute-start(f32[2,2,256,256]{3,2,1,0:T(8,128)} %get-tuple-element.525), channel_id=1, source_target_pairs={{16,0},{32,16},{48,32},{64,48},{80,64},{96,80},{112,96},{17,1},{33... | collective-permute-start | bytes 3145736 | tf_op jit(solution)/shard_map/while/body/eval_jaxpr/ppermute | solution.py:19
  513.6 22.5 %collective-permute-start.1 = (f32[2,2,256,256]{3,2,1,0:T(8,128)}, f32[2,2,256,256]{3,2,1,0:T(8,128)}, u32[]{:S(2)}, u32[]{:S(2)}) collective-permute-start(f32[2,2,256,256]{3,2,1,0:T(8,128)} %get-tuple-element.525), channel_id=1, source_target_pairs={{16,0},{32,16},{48,32},{64,48},{80,64},{96,80},{112,96},{17,1},{33... | collective-permute-start | bytes 3145736 | tf_op jit(solution)/shard_map/while/body/eval_jaxpr/ppermute | solution.py:19
  536.0 148.4 %collective-permute-start.1 = (f32[2,2,256,256]{3,2,1,0:T(8,128)}, f32[2,2,256,256]{3,2,1,0:T(8,128)}, u32[]{:S(2)}, u32[]{:S(2)}) collective-permute-start(f32[2,2,256,256]{3,2,1,0:T(8,128)} %get-tuple-element.525), channel_id=1, source_target_pairs={{16,0},{32,16},{48,32},{64,48},{80,64},{96,80},{112,96},{17,1},{33... | collective-permute-start | bytes 3145736 | tf_op jit(solution)/shard_map/while/body/eval_jaxpr/ppermute | solution.py:19
  745.9 7.8 copy-start.2
  791.9 9.3 %slice-start.5 = ((s8[4718592]{0:T(1024)(128)(4,1)}), s8[4194304]{0:T(1024)(128)(4,1)S(1)}, s32[]{:S(2)}) async-start(s8[4718592]{0:T(1024)(128)(4,1)} %bitcast.496), calls=%async_computation.6 | async-start | bytes 8388608
  (39 other events, 128.3 us)
Sparse Core Ops, SparseCore 0:
  10.4 151.3 all-gather.1
where the time goes:
time: 828 us; the launch traced here: 817 us
  waiting for transfers between devices  441 us (53%)
  matrix products  165 us (20%)
  local copies, waits for them, and re-layouts  106 us (13%)
  starting transfers between devices  62.9 us (8%)
  other arithmetic  26.1 us (3%)
  between operations  15.4 us (2%)
    ppermute x14, waiting for transfers between devices, passed_along(): lax.ppermute(value, axis, [(source, source + steps) for source in range(l...  349 us
    dot_general x52, matrix products, product(): jnp.einsum(pattern, left_factor, right_factor, preferred_element_type=jnp...  99.5 us
    all_gather x1, waiting for transfers between devices, body(): received_piece = lax.all_gather(prev_lesser, 'energy', axis=1, tiled=True)  90.9 us
    ppermute x14, starting transfers between devices, passed_along(): lax.ppermute(value, axis, [(source, source + steps) for source in range(l...  62.8 us
    dot_general x1, matrix products, body(): jnp.einsum('c,cpak->pak', weights, received_piece[0], precision=FULL_PREC...  40.3 us
    squeeze x2, local copies, waits for them, and re-layouts, conjugate_product(): left_factor[0]  18.1 us
    squeeze x2, local copies, waits for them, and re-layouts, conjugate_product(): left_factor[1]  18.1 us
    another operation x1, local copies, waits for them, and re-layouts, diagonal_blocks(): shaped = green_fn.reshape(2, NBLK, BLK, NBLK, BLK)  17.9 us
  transfers between devices with their start and end apart: 15, of which 15 were waited for; matrix products, arithmetic and copies ran while one was open for 8% of the time, Pallas kernels for 0%

commit v1 on v0

v1 whole, which is shorter than its diff:
```python
import functools

import jax
import jax.numpy as jnp
from jax import lax
from jax.experimental import pallas as pl
from jax.experimental.pallas import tpu as pltpu
from jax.sharding import PartitionSpec as P

SLAB_ORBITALS = 1536
BW = 256
BLK = 128
NBLK = 12
NBW = 2
PAIRS = SLAB_ORBITALS // BW
HALF = 4

FULL_PRECISION = lax.Precision.HIGHEST
MESH = pl.DeviceIdType.MESH
VMEM_LIMIT = 58 * 1024 * 1024
NN = (((1,), (0,)), ((), ()))
NT = (((1,), (1,)), ((), ()))

f32 = jnp.float32
bf16 = jnp.bfloat16


def dot(left, right, dims=NN):
    return lax.dot_general(left, right, dims, preferred_element_type=f32)


def split(value):
    high = value.astype(bf16)
    return high, (value - high.astype(f32)).astype(bf16)


def turned(value):
    width = value.shape[1] // 2
    return jnp.concatenate([-value[:, width:], value[:, :width]], axis=1)


def doubled(value):
    return jnp.concatenate([value, turned(value)], axis=0)


def product(left, right, dims=NN):
    left_high, left_low = split(left)
    right_high, right_low = split(right)
    main = doubled(right_high)
    return (
        dot(left_high, main, dims) + dot(left_low, main, dims) + dot(left_high, doubled(right_low), dims)
    )


def exact_left(left, right, dims=NN):
    right_high, right_low = split(right)
    return dot(left, doubled(right_high), dims) + dot(left, doubled(right_low), dims)


def exact_right(left, right, dims=NN):
    left_high, left_low = split(left)
    main = doubled(right)
    return dot(left_high, main, dims) + dot(left_low, main, dims)


def real_left(matrix, value):
    matrix_high, matrix_low = split(matrix)
    value_high, value_low = split(value)
    return dot(matrix_high, value_high) + dot(matrix_high, value_low) + dot(matrix_low, value_high)


def real_right(value, matrix):
    matrix_high, matrix_low = split(matrix)
    parts = []
    for part in (value[:, :BW], value[:, BW:]):
        high, low = split(part)
        parts.append(dot(high, matrix_high) + dot(low, matrix_high) + dot(high, matrix_low))
    return jnp.concatenate(parts, axis=1)


def beside(ref):
    return jnp.concatenate([ref[0], ref[1]], axis=1)


def adjoint(value):
    return jnp.concatenate([value[:, :BW].T, -value[:, BW:].T], axis=1)


class Place:
    def __init__(self):
        slab = lax.axis_index("slab")
        self.half = slab // HALF
        self.z = slab % HALF
        base = self.half * HALF
        self.right = base + (self.z + 1) % HALF
        self.left = base + (self.z + HALF - 1) % HALF
        self.across = (slab + HALF) % (2 * HALF)


def enter(place):
    barrier = pltpu.get_barrier_semaphore()
    for other in (place.left, place.right, place.across):
        pl.semaphore_signal(barrier, inc=1, device_id={"slab": other}, device_id_type=MESH)
    pl.semaphore_wait(barrier, 3)


class Gather:
    def __init__(self, place, slots, send, recv):
        z = place.z
        low, high = pl.ds(0, BW // 2), pl.ds(BW // 2, BW // 2)
        before, after, opposite = (z + 3) % HALF, (z + 1) % HALF, (z + 2) % HALF

        def copy(index, slot, rows, target):
            part = slots.at[slot, rows]
            return pltpu.make_async_remote_copy(
                src_ref=part,
                dst_ref=part,
                send_sem=send.at[index],
                recv_sem=recv.at[index],
                device_id={"slab": target},
                device_id_type=MESH,
            )

        self.first = [
            copy(0, z, low, place.right),
            copy(1, z, high, place.left),
            copy(2, z, high, place.right),
            copy(3, z, low, place.left),
        ]
        self.arrive = [
            copy(0, before, low, place.right),
            copy(1, after, high, place.left),
            copy(2, before, high, place.right),
            copy(3, after, low, place.left),
        ]
        self.relay = [copy(4, before, low, place.right), copy(5, after, high, place.left)]
        self.last = [copy(4, opposite, low, place.right), copy(5, opposite, high, place.left)]

    def start(self):
        for item in self.first:
            item.start()

    def forward(self):
        for index in (0, 1):
            self.arrive[index].wait_recv()
            self.relay[index].start()

    def finish(self):
        for item in self.arrive[2:] + self.last:
            item.wait_recv()
        for item in self.first + self.relay:
            item.wait_send()


def crossing(place, source, target, send, recv):
    return pltpu.make_async_remote_copy(
        src_ref=source,
        dst_ref=target,
        send_sem=send,
        recv_sem=recv,
        device_id={"slab": place.across},
        device_id_type=MESH,
    )


def early_kernel(
    g_rl, g_lr, g_ll, coupling, coupling_t,
    transfer, inward, through, far,
    corner, run, own, incoming, send, recv, cross_send, cross_recv,
):
    place = Place()
    z, half = place.z, place.half
    enter(place)
    turn = [Gather(place, ref, send.at[i], recv.at[i]) for i, ref in enumerate((transfer, inward, corner))]
    c_high, c_low = split(coupling[...])
    t_high, t_low = split(coupling_t[...])
    value = beside(g_rl)
    transfer[z] = dot(t_high, value) + dot(t_low, value)
    turn[0].start()
    parts = [dot(g_lr[i], c_high) + dot(g_lr[i], c_low) for i in (0, 1)]
    inward[z] = jnp.concatenate(parts, axis=1)
    turn[1].start()
    corner[z] = beside(g_ll).astype(f32)
    turn[2].start()
    for item in turn:
        item.forward()
    for item in turn:
        item.finish()

    own[...] = jnp.zeros_like(own)

    def step(index, _):
        j = HALF - 1 - index

        @pl.when(j == z)
        def _():
            own[...] = run[...]

        run[...] = corner[j] + product(product(inward[j], run[...]), transfer[j])
        return 0

    cross = crossing(place, run, incoming, cross_send, cross_recv)

    @pl.when(half == 1)
    def _():
        run[...] = corner[HALF - 1]

    @pl.when(half == 0)
    def _():
        cross.wait_recv()
        run[...] = incoming[...]

    lax.fori_loop(half, jnp.where(half == 1, HALF, HALF - 1 - z), step, 0)

    @pl.when(half == 1)
    def _():
        cross.start()
        cross.wait_send()

    @pl.when(half == 0)
    def _():
        own[...] = run[...]

    value = own[...]
    outer = real_right(value, coupling_t[...])
    through[...] = product(inward[z], outer)
    far[...] = real_left(coupling[...], outer).astype(bf16)


def sweep_kernel(
    transfer, inward, through, coupling, coupling_t, g_ll, g_rl, outer_rr, outer_rl, outer_ll,
    state, far,
    source, driven, run, own, incoming, send, recv, cross_send, cross_recv,
):
    place = Place()
    z, half = place.z, place.half
    enter(place)
    turn = Gather(place, source, send.at[0], recv.at[0])
    source[z] = real_left(coupling_t[...], real_right(beside(outer_rr), coupling[...]))
    turn.start()
    turn.forward()
    turn.finish()

    own[...] = jnp.zeros_like(own)

    def forward_step(j, _):
        @pl.when(j == z)
        def _():
            own[...] = run[...]

        factor = transfer[j]
        run[...] = product(product(factor, run[...]), factor, NT) + source[j]
        return 0

    up = crossing(place, run, incoming, cross_send.at[0], cross_recv.at[0])

    @pl.when(half == 0)
    def _():
        run[...] = source[0]

    @pl.when(half == 1)
    def _():
        up.wait_recv()
        run[...] = incoming[...]

    lax.fori_loop(1 - half, jnp.where(half == 0, HALF, z), forward_step, 0)

    @pl.when(half == 0)
    def _():
        up.start()

    @pl.when(half == 1)
    def _():
        own[...] = run[...]

    value = own[...]
    state[...] = value.astype(bf16)
    left = beside(g_ll)
    tail = exact_right(value, left, NT)
    right = exact_left(jnp.concatenate([left, beside(g_rl)], axis=0), tail)
    mixed = product(through[...], beside(outer_rl) + right[BW:])
    turn = Gather(place, driven, send.at[1], recv.at[1])
    driven[z] = beside(outer_ll) + right[:BW] + mixed + adjoint(mixed)
    turn.start()
    turn.forward()
    turn.finish()

    @pl.when(half == 0)
    def _():
        up.wait_send()

    own[...] = jnp.zeros_like(own)

    def backward_step(index, _):
        j = HALF - 1 - index

        @pl.when(j == z)
        def _():
            own[...] = run[...]

        factor = inward[j]
        run[...] = product(product(factor, run[...]), factor, NT) + driven[j]
        return 0

    down = crossing(place, run, incoming, cross_send.at[1], cross_recv.at[1])

    @pl.when(half == 1)
    def _():
        run[...] = driven[HALF - 1]

    @pl.when(half == 0)
    def _():
        down.wait_recv()
        run[...] = incoming[...]

    lax.fori_loop(half, jnp.where(half == 1, HALF, HALF - 1 - z), backward_step, 0)

    @pl.when(half == 1)
    def _():
        down.start()

    @pl.when(half == 0)
    def _():
        own[...] = run[...]

    far[...] = real_left(coupling[...], real_right(own[...], coupling_t[...])).astype(bf16)

    @pl.when(half == 1)
    def _():
        down.wait_send()


def local_kernel(green, sigma, outer_right, outer_left, outer_blocks, scaled):
    rows = 512

    def scale(n, _):
        columns = pl.ds(pl.multiple_of(n * BLK, BLK), BLK)
        real, imag = sigma[0, columns, :], sigma[1, columns, :]
        factor = jnp.concatenate(
            [jnp.concatenate([real, imag], axis=1), jnp.concatenate([-imag, real], axis=1)], axis=0
        )
        for start in range(0, SLAB_ORBITALS, rows):
            span = pl.ds(start, rows)
            piece = jnp.concatenate([green[0, span, columns], green[1, span, columns]], axis=1)
            result = dot(piece, factor).astype(bf16)
            scaled[0, span, columns] = result[:, :BLK]
            scaled[1, span, columns] = result[:, BLK:]
            scaled[2, span, columns] = -result[:, :BLK]
        return 0

    lax.fori_loop(0, NBLK, scale, 0)
    last = pl.ds(SLAB_ORBITALS - BW, BW)

    def against(left_rows, right_rows):
        first = scaled[0:2, left_rows, :].reshape(2 * BW, SLAB_ORBITALS)
        second = scaled[1:3, left_rows, :].reshape(2 * BW, SLAB_ORBITALS)
        total = dot(first, green[0, right_rows, :], NT) + dot(second, green[1, right_rows, :], NT)
        return total.reshape(2, BW, BW)

    def pair(m, _):
        span = pl.ds(pl.multiple_of(m * BW, BW), BW)
        outer_right[m] = against(last, span)
        local = against(span, span)
        first = pl.ds(pl.multiple_of(m * BW, BW), BLK)
        second = pl.ds(pl.multiple_of(m * BW + BLK, BLK), BLK)
        outer_blocks[:, first, :] = local[:, :BLK, :BLK]
        outer_blocks[:, second, :] = local[:, BLK:, BLK:]

        @pl.when(m == 0)
        def _():
            outer_left[...] = local

        return 0

    lax.fori_loop(0, PAIRS, pair, 0)


def final_kernel(
    green, state, retarded_far, lesser_far, outer_right, outer_blocks,
    retarded_out, lesser_out,
    coupled, lesser_weighted, retarded_weighted,
):
    rows = 512
    left = pl.ds(0, BW)
    last = pl.ds(SLAB_ORBITALS - BW, BW)
    state_factor = doubled(state[...])
    retarded_factor = doubled(retarded_far[...])
    lesser_factor = doubled(lesser_far[...])
    for start in range(0, SLAB_ORBITALS, rows):
        span = pl.ds(start, rows)
        piece = jnp.concatenate([green[0, span, left], green[1, span, left]], axis=1)
        result = dot(piece, state_factor).astype(bf16)
        coupled[0, span, :] = result[:, :BW]
        coupled[1, span, :] = result[:, BW:]
        coupled[2, span, :] = -result[:, :BW]
        piece = jnp.concatenate([green[0, span, last], green[1, span, last]], axis=1)
        retarded_weighted[span, :] = dot(piece, retarded_factor).astype(bf16)
        result = dot(piece, lesser_factor).astype(bf16)
        lesser_weighted[0, span, :] = result[:, :BW]
        lesser_weighted[1, span, :] = result[:, BW:]
        lesser_weighted[2, span, :] = -result[:, :BW]

    def against(values, left_rows, right_rows, columns):
        first = values[0:2, left_rows, :].reshape(2 * BW, BW)
        second = values[1:3, left_rows, :].reshape(2 * BW, BW)
        total = dot(first, green[0, right_rows, columns], NT) + dot(second, green[1, right_rows, columns], NT)
        return total.reshape(2, BW, BW)

    def pair(m, _):
        span = pl.ds(pl.multiple_of(m * BW, BW), BW)
        far_right = (outer_right[m] + against(coupled, last, span, left)).astype(bf16)
        weighted = retarded_weighted[span, :]
        retarded = dot(weighted, doubled(jnp.concatenate([green[0, last, span], green[1, last, span]], axis=1)))
        mixed = dot(weighted, doubled(jnp.concatenate([far_right[0], far_right[1]], axis=1)))
        lesser = against(coupled, span, span, left) + against(lesser_weighted, span, span, last)
        for k in (0, 1):
            start = pl.multiple_of(m * BW + k * BLK, BLK)
            block = pl.ds(start, BLK)
            here = slice(k * BLK, (k + 1) * BLK)
            for part in (0, 1):
                there = slice(part * BW + k * BLK, part * BW + (k + 1) * BLK)
                retarded_out[part, block, :] = green[part, block, block].astype(f32) + retarded[here, there]
                mix = mixed[here, there]
                mirrored = mix.T if part == 0 else -mix.T
                lesser_out[part, block, :] = outer_blocks[part, block, :] + lesser[part, here, here] + mix + mirrored
        return 0

    lax.fori_loop(0, PAIRS, pair, 0)


def whole(count):
    return [pl.BlockSpec(memory_space=pltpu.VMEM)] * count


def shape(dims, dtype=f32):
    return jax.ShapeDtypeStruct(dims, dtype)


WIDE = (BW, 2 * BW)


def early(g_rl, g_lr, g_ll, coupling, coupling_t):
    return pl.pallas_call(
        early_kernel,
        out_shape=[shape((HALF,) + WIDE), shape((HALF,) + WIDE), shape(WIDE), shape(WIDE, bf16)],
        in_specs=whole(5),
        out_specs=whole(4),
        scratch_shapes=[
            pltpu.VMEM((HALF,) + WIDE, f32),
            pltpu.VMEM(WIDE, f32),
            pltpu.VMEM(WIDE, f32),
            pltpu.VMEM(WIDE, f32),
            pltpu.SemaphoreType.DMA((3, 6)),
            pltpu.SemaphoreType.DMA((3, 6)),
            pltpu.SemaphoreType.DMA,
            pltpu.SemaphoreType.DMA,
        ],
        compiler_params=pltpu.CompilerParams(
            collective_id=0, has_side_effects=True, vmem_limit_bytes=VMEM_LIMIT
        ),
    )(g_rl, g_lr, g_ll, coupling, coupling_t)


def sweep(*operands):
    return pl.pallas_call(
        sweep_kernel,
        out_shape=[shape(WIDE, bf16), shape(WIDE, bf16)],
        in_specs=whole(len(operands)),
        out_specs=whole(2),
        scratch_shapes=[
            pltpu.VMEM((HALF,) + WIDE, f32),
            pltpu.VMEM((HALF,) + WIDE, f32),
            pltpu.VMEM(WIDE, f32),
            pltpu.VMEM(WIDE, f32),
            pltpu.VMEM(WIDE, f32),
            pltpu.SemaphoreType.DMA((2, 6)),
            pltpu.SemaphoreType.DMA((2, 6)),
            pltpu.SemaphoreType.DMA((2,)),
            pltpu.SemaphoreType.DMA((2,)),
        ],
        compiler_params=pltpu.CompilerParams(
            collective_id=1, has_side_effects=True, vmem_limit_bytes=VMEM_LIMIT
        ),
    )(*operands)


def local_terms(green, sigma):
    return pl.pallas_call(
        local_kernel,
        out_shape=[
            shape((PAIRS, 2, BW, BW)),
            shape((2, BW, BW)),
            shape((2, SLAB_ORBITALS, BLK)),
        ],
        in_specs=whole(2),
        out_specs=whole(3),
        scratch_shapes=[pltpu.VMEM((3, SLAB_ORBITALS, SLAB_ORBITALS), bf16)],
        compiler_params=pltpu.CompilerParams(vmem_limit_bytes=VMEM_LIMIT),
    )(green, sigma)


def final_terms(*operands):
    return pl.pallas_call(
        final_kernel,
        out_shape=[shape((2, SLAB_ORBITALS, BLK)), shape((2, SLAB_ORBITALS, BLK))],
        in_specs=whole(len(operands)),
        out_specs=whole(2),
        scratch_shapes=[
            pltpu.VMEM((3, SLAB_ORBITALS, BW), bf16),
            pltpu.VMEM((3, SLAB_ORBITALS, BW), bf16),
            pltpu.VMEM((SLAB_ORBITALS, 2 * BW), bf16),
        ],
        compiler_params=pltpu.CompilerParams(vmem_limit_bytes=VMEM_LIMIT),
    )(*operands)


def dense_coupling(block_index, block_values):
    positions = jnp.arange(NBW, dtype=jnp.int32)[None, :]
    row_select = (block_index[:, 0:1] == positions).astype(jnp.float32)
    column_select = (block_index[:, 1:2] == positions).astype(jnp.float32)
    dense = jnp.einsum(
        "br,bc,bij->ricj", row_select, column_select, block_values, precision=FULL_PRECISION
    )
    return dense.reshape(BW, BW)


def partner_weights(targets, sources, phonon_shift, phonon_weight):
    target_column = jnp.asarray(targets)[..., None]
    source_column = jnp.asarray(sources)[..., None]
    emission = jnp.where(source_column == target_column + phonon_shift, phonon_weight[0], 0.0)
    absorption = jnp.where(source_column == target_column - phonon_shift, phonon_weight[1], 0.0)
    return jnp.sum(emission + absorption, axis=-1)


def slab_work(green, sigma, coupling):
    lead, tail = slice(0, BW), slice(SLAB_ORBITALS - BW, SLAB_ORBITALS)
    g_ll, g_rl, g_lr = green[:, lead, lead], green[:, tail, lead], green[:, lead, tail]
    coupling_t = coupling.T
    transfer, inward, through, retarded_far = early(g_rl, g_lr, g_ll, coupling, coupling_t)
    outer_right, outer_left, outer_blocks = local_terms(green, sigma)
    state, lesser_far = sweep(
        transfer, inward, through, coupling, coupling_t, g_ll, g_rl,
        outer_right[PAIRS - 1], outer_right[0], outer_left,
    )
    return final_terms(green, state, retarded_far, lesser_far, outer_right, outer_blocks)


def body(green_ret, prev_lesser, coupling_index, coupling_values, phonon_shift, phonon_weight):
    green = green_ret[0, 0]
    coupling = dense_coupling(coupling_index[0], coupling_values[0])
    my_energy = lax.axis_index("energy")
    received = lax.all_gather(prev_lesser[0, 0], "energy", axis=0, tiled=False)
    sources = jnp.arange(received.shape[0], dtype=jnp.int32)
    weights = partner_weights(my_energy, sources, phonon_shift, phonon_weight)
    sigma = sum(weights[f] * received[f] for f in range(received.shape[0])).astype(bf16)
    retarded, lesser = slab_work(green, sigma, coupling)
    return retarded[None, None], lesser[None, None]


def solution(mesh):
    placed = (
        P("slab", "energy", None, None, None),
        P("slab", "energy", None, None, None),
        P("slab", None, None),
        P("slab", None, None, None),
        P(),
        P(),
    )
    return jax.shard_map(
        body,
        mesh=mesh,
        in_specs=placed,
        out_specs=(P("slab", "energy", None, None, None), P("slab", "energy", None, None, None)),
        check_vma=False,
    )
```

time: 828 us -> 323 us (0.39); the launches traced: 817 us -> 322 us
  waiting for transfers between devices: 441 us -> 58.4 us
  Pallas kernels: 0 us -> 222 us
  matrix products: 165 us -> 0.8 us
  local copies, waits for them, and re-layouts: 106 us -> 6.19 us
  starting transfers between devices: 62.9 us -> 0.04 us
    ppermute x14 -> x0, waiting for transfers between devices: 349 us -> none  [passed_along(): lax.ppermute(value, axis, [(source, source + steps) for source in range(l...]
    pallas_call x0 -> x4, Pallas kernels: none -> 222 us  [the longest x1 94.5 us: sweep(): pl.pallas_call(sweep_kernel, out_shape=[shape(WIDE, bf16), shape(WIDE, bf...]
    dot_general x82 -> x0, matrix products: 164 us -> none  [the longest x52 99.5 us: product(): jnp.einsum(pattern, left_factor, right_factor, preferred_element_type=jnp...]
    ppermute x14 -> x0, starting transfers between devices: 62.8 us -> none  [passed_along(): lax.ppermute(value, axis, [(source, source + steps) for source in range(l...]
    squeeze x4 -> x1, local copies, waits for them, and re-layouts: 36.3 us -> 2.26 us  [slab_work(): outer_right[0]]
    all_gather x1, waiting for transfers between devices: 90.9 us -> 57.7 us  [body(): received = lax.all_gather(prev_lesser[0, 0], 'energy', axis=0, tiled=False)]
    another operation x1 -> x0, local copies, waits for them, and re-layouts: 17.9 us -> none  [diagonal_blocks(): shaped = green_fn.reshape(2, NBLK, BLK, NBLK, BLK)]
    unnamed x97 -> x11, local copies, waits for them, and re-layouts: 16.3 us -> 0.19 us
  transfers between devices with their start and end apart: 15 -> 1, of which waited for: 15 -> 1; matrix products, arithmetic and copies ran while one was open for 8% -> 1% of each run, Pallas kernels for 0% -> 28%
where the time goes in v1:
time: 323 us; the launch traced here: 322 us
  Pallas kernels  222 us (69%)
  waiting for transfers between devices  58.4 us (18%)
  other arithmetic  20.4 us (6%)
  between operations  14.2 us (4%)
  local copies, waits for them, and re-layouts  6.19 us (2%)
    pallas_call x1, Pallas kernels, sweep(): pl.pallas_call(sweep_kernel, out_shape=[shape(WIDE, bf16), shape(WIDE, bf...  94.5 us
    pallas_call x1, Pallas kernels, early(): pl.pallas_call(early_kernel, out_shape=[shape((HALF,) + WIDE), shape((HAL...  91.3 us
    all_gather x1, waiting for transfers between devices, body(): received = lax.all_gather(prev_lesser[0, 0], 'energy', axis=0, tiled=False)  57.7 us
    pallas_call x1, Pallas kernels, local_terms(): pl.pallas_call(local_kernel, out_shape=[shape((PAIRS, 2, BW, BW)), shape(...  21.8 us
    convert_element_type x1, other arithmetic, body(): sum((weights[f] * received[f] for f in range(received.shape[0])))  20.3 us
    pallas_call x1, Pallas kernels, final_terms(): pl.pallas_call(final_kernel, out_shape=[shape((2, SLAB_ORBITALS, BLK)), s...  14.9 us
  transfers between devices with their start and end apart: 1, of which 1 were waited for; matrix products, arithmetic and copies ran while one was open for 1% of the time, Pallas kernels for 28%

profile of v1, /device:TPU:0, one launch (start us, length us, event | category | flops | bytes accessed | tf_op | source)
XLA Modules:
  0.0 322.4 jit_solution(9530475779497424995)
XLA Ops:
  7.2 0.0 copy-start.2
  7.2 0.0 copy-start.1
  7.2 0.0 all-gather.3.cloned.1.call-start
  7.2 0.7 all-gather.3.cloned.1.call-update
  7.9 0.0 copy-done.2
  8.0 0.2 copy-done.1
  8.1 0.8 convolution_bitcast_fusion
  8.9 0.2 copy.17
  9.1 0.0 copy-start
  9.1 0.8 copy.18.coupling
  9.9 0.0 copy-start.4
  10.0 2.0 fusion.34
  12.0 0.0 copy-done
  12.0 91.3 %shard_map.77 = (f32[4,256,512]{2,1,0:T(8,128)}, f32[4,256,512]{2,1,0:T(8,128)}, f32[256,512]{1,0:T(8,128)}, bf16[256,512]{1,0:T(8,128)(2,1)}) custom-call(bf16[2,256,256]{2,1,0:T(8,128)(2,1)} %get-tuple-element.26.g_rl, bf16[2,256,256]{2,1,0:T(8,128)(2,1)} %get-tuple-element.25.g_lr, bf16[2,256,256]{2,1,0:T(8,128)(2,1)} %get-tuple-element.24.g_ll, ...), custom_call_target="tpu_custom_call" | custom-call | tf_op jit(solution)/shard_map/pallas_call | solution.py:443
  103.3 0.0 copy-done.4
  103.3 0.0 copy-done.3
  103.3 0.1 add_reduce_fusion
  103.4 0.7 fusion.35
  104.1 57.7 %all-gather.3.cloned.1.call-done = f32[16,1,2,1536,128]{4,3,2,1,0:T(8,128)} async-done(((f32[1,1,2,1536,128]{4,3,2,1,0:T(8,128)}), f32[16,1,2,1536,128]{4,3,2,1,0:T(8,128)}) %all-gather.3.cloned.1.call-update) | async-done | bytes 25165840 | tf_op jit(solution)/shard_map/all_gather | solution.py:552
  161.8 20.3 %fusion.2.sigma = bf16[2,1536,128]{2,1,0:T(8,128)(2,1)} fusion(f32[16,1,2,1536,128]{4,3,2,1,0:T(8,128)} %all-gather.3.cloned.1.call-done, f32[]{:T(128)} %bitcast.37, f32[]{:T(128)} %bitcast.35, f32[]{:T(128)} %bitcast.33, f32[]{:T(128)} %bitcast.31, f32[]{:T(128)} %bitcast.29, f32[]{:T(128)} %bitcast.27, f32[]{:T(128)} %bitcast.24, f32[]{:T(128)} %bitcast.22, ...), kind=kLoop, calls=%fused_computation.3 | loop fusion | flops 12582912 | bytes 25952320 | tf_op jit(solution)/shard_map/convert_element_type | solution.py:555
  182.2 21.8 %shard_map.78 = (f32[6,2,256,256]{3,2,1,0:T(8,128)}, f32[2,256,256]{2,1,0:T(8,128)}, f32[2,1536,128]{2,1,0:T(8,128)}) custom-call(bf16[2,1536,1536]{2,1,0:T(8,128)(2,1)} %bitcast.120, bf16[2,1536,128]{2,1,0:T(8,128)(2,1)} %fusion.2.sigma), custom_call_target="tpu_custom_call" | custom-call | tf_op jit(solution)/shard_map/pallas_call | solution.py:488
  204.0 2.3 slice_bitcast_fusion
  206.2 94.5 %shard_map.79 = (bf16[256,512]{1,0:T(8,128)(2,1)}, bf16[256,512]{1,0:T(8,128)(2,1)}) custom-call(f32[4,256,512]{2,1,0:T(8,128)} %get-tuple-element.13.transfer, f32[4,256,512]{2,1,0:T(8,128)} %get-tuple-element.14.inward, f32[256,512]{1,0:T(8,128)} %get-tuple-element.15.through, f32[256,256]{1,0:T(8,128)} %copy.18.coupling, f32[256,256]{1,0:T(8,128)} %bitcast.124, ...), custom_call_target="tpu_custom_call" | custom-call | tf_op jit(solution)/shard_map/pallas_call | solution.py:465
  300.7 14.9 %shard_map.80 = (f32[2,1536,128]{2,1,0:T(8,128)}, f32[2,1536,128]{2,1,0:T(8,128)}) custom-call(bf16[2,1536,1536]{2,1,0:T(8,128)(2,1)} %bitcast.121, bf16[256,512]{1,0:T(8,128)(2,1)} %get-tuple-element.18.state, bf16[256,512]{1,0:T(8,128)(2,1)} %get-tuple-element.19.retarded_far, bf16[256,512]{1,0:T(8,128)(2,1)} %get-tuple-element.20.lesser_far, ...), custom_call_target="tpu_custom_call" | custom-call | tf_op jit(solution)/shard_map/pallas_call | solution.py:503
  (6 shorter events, 0.0 us)
Async XLA Ops:
  7.2 0.8 copy-start.2
  7.2 0.9 copy-start.1
  7.2 154.7 %all-gather.3.cloned.1.call-start = ((), (), s32[]{:S(2)}) async-start(), calls=%async_computation | async-start | bytes 26738688 | tf_op jit(solution)/shard_map/all_gather | solution.py:552
  9.1 2.9 copy-start
  9.9 93.3 %copy-start.4 = (s32[3]{0:T(128)S(1)}, s32[3]{0:T(128)}, u32[]{:S(2)}) copy-start(s32[3]{0:T(128)} %param.10) | copy-start | bytes 40
  9.9 93.4 %copy-start.3 = (f32[2,3]{1,0:T(2,128)S(1)}, f32[2,3]{1,0:T(2,128)}, u32[]{:S(2)}) copy-start(f32[2,3]{1,0:T(2,128)} %param.11) | copy-start | bytes 76
Sparse Core Ops, SparseCore 0:
  10.4 151.3 all-gather.2

commit v2 on v1

--- a/solution.py
+++ b/solution.py
@@ -52,17 +52,6 @@
     )
 
 
-def exact_left(left, right, dims=NN):
-    right_high, right_low = split(right)
-    return dot(left, doubled(right_high), dims) + dot(left, doubled(right_low), dims)
-
-
-def exact_right(left, right, dims=NN):
-    left_high, left_low = split(left)
-    main = doubled(right)
-    return dot(left_high, main, dims) + dot(left_low, main, dims)
-
-
 def real_left(matrix, value):
     matrix_high, matrix_low = split(matrix)
     value_high, value_low = split(value)
@@ -88,20 +77,32 @@
 
 class Place:
     def __init__(self):
-        slab = lax.axis_index("slab")
+        slab, energy = lax.axis_index("slab"), lax.axis_index("energy")
         self.half = slab // HALF
         self.z = slab % HALF
         base = self.half * HALF
-        self.right = base + (self.z + 1) % HALF
-        self.left = base + (self.z + HALF - 1) % HALF
-        self.across = (slab + HALF) % (2 * HALF)
-
-
-def enter(place):
+        self.right = {"slab": base + (self.z + 1) % HALF}
+        self.left = {"slab": base + (self.z + HALF - 1) % HALF}
+        other_half = (slab + HALF) % (2 * HALF)
+        flipped = energy + 2 - 4 * (energy // 2 % 2)
+        self.across = {"slab": other_half}
+        self.across_flipped = {"slab": other_half, "energy": flipped}
+        self.core = {"energy": energy + 1 - 2 * (energy % 2)}
+        self.x_next = {"energy": (energy + 4) % 16}
+        self.x_before = {"energy": (energy + 12) % 16}
+
+
+def enter(others):
     barrier = pltpu.get_barrier_semaphore()
-    for other in (place.left, place.right, place.across):
-        pl.semaphore_signal(barrier, inc=1, device_id={"slab": other}, device_id_type=MESH)
-    pl.semaphore_wait(barrier, 3)
+    for other in others:
+        pl.semaphore_signal(barrier, inc=1, device_id=other, device_id_type=MESH)
+    pl.semaphore_wait(barrier, len(others))
+
+
+def sending(source, target, send, recv, device):
+    return pltpu.make_async_remote_copy(
+        src_ref=source, dst_ref=target, send_sem=send, recv_sem=recv, device_id=device, device_id_type=MESH
+    )
 
 
 class Gather:
@@ -112,14 +113,7 @@
 
         def copy(index, slot, rows, target):
             part = slots.at[slot, rows]
-            return pltpu.make_async_remote_copy(
-                src_ref=part,
-                dst_ref=part,
-                send_sem=send.at[index],
-                recv_sem=recv.at[index],
-                device_id={"slab": target},
-                device_id_type=MESH,
-            )
+            return sending(part, part, send.at[index], recv.at[index], target)
 
         self.first = [
             copy(0, z, low, place.right),
@@ -152,26 +146,62 @@
             item.wait_send()
 
 
-def crossing(place, source, target, send, recv):
-    return pltpu.make_async_remote_copy(
-        src_ref=source,
-        dst_ref=target,
-        send_sem=send,
-        recv_sem=recv,
-        device_id={"slab": place.across},
-        device_id_type=MESH,
-    )
-
-
-def early_kernel(
-    g_rl, g_lr, g_ll, coupling, coupling_t,
-    transfer, inward, through, far,
-    corner, run, own, incoming, send, recv, cross_send, cross_recv,
+CHUNKS = 4
+STACKED = 2 * SLAB_ORBITALS
+CHUNK = STACKED // CHUNKS
+PART = CHUNK // 2
+
+
+def phonon_kernel(
+    weights, previous, g_rl, g_lr, g_ll, coupling, coupling_t,
+    sigma, transfer, inward, corner,
+    others, relay, two_away, after, before, passing, from_before, from_after, mine,
+    z_send, z_recv, y_send, y_recv, core_send, core_recv, x_send, x_recv,
 ):
     place = Place()
-    z, half = place.z, place.half
-    enter(place)
-    turn = [Gather(place, ref, send.at[i], recv.at[i]) for i, ref in enumerate((transfer, inward, corner))]
+    enter([place.left, place.right, place.across, place.across_flipped, place.core, place.x_next, place.x_before])
+    z = place.z
+
+    def low(c):
+        return pl.ds(c * CHUNK, PART)
+
+    def high(c):
+        return pl.ds(c * CHUNK + PART, PART)
+
+    def full(c):
+        return pl.ds(c * CHUNK, CHUNK)
+
+    steps = range(CHUNKS)
+
+    def over_y(kind, source, target, device):
+        return [sending(source(c), target(c), y_send.at[kind, c], y_recv.at[kind, c], device) for c in steps]
+
+    def over_core(kind, source, target):
+        return [sending(source(c), target(c), core_send.at[kind, c], core_recv.at[kind, c], place.core) for c in steps]
+
+    def over_x(kind, source, target, device):
+        return [sending(source(c), target(c), x_send.at[kind, c], x_recv.at[kind, c], device) for c in steps]
+
+    hop_a = over_y(0, lambda c: previous.at[low(c)], lambda c: relay.at[0, c], place.across)
+    end_a = over_y(1, lambda c: relay.at[0, c], lambda c: others.at[1, low(c)], place.across_flipped)
+    hop_b = over_y(2, lambda c: previous.at[high(c)], lambda c: relay.at[1, c], place.across_flipped)
+    end_b = over_y(3, lambda c: relay.at[1, c], lambda c: others.at[1, high(c)], place.across)
+    core_own = over_core(0, lambda c: previous.at[full(c)], lambda c: others.at[0, full(c)])
+    core_more = over_core(1, lambda c: others.at[1, full(c)], lambda c: others.at[2, full(c)])
+    two_low = over_x(0, lambda c: two_away.at[low(c)], lambda c: passing.at[0, c], place.x_next)
+    two_high = over_x(1, lambda c: two_away.at[high(c)], lambda c: passing.at[1, c], place.x_before)
+    after_high = over_x(2, lambda c: after.at[high(c)], lambda c: from_before.at[high(c)], place.x_next)
+    before_low = over_x(3, lambda c: before.at[low(c)], lambda c: from_after.at[low(c)], place.x_before)
+    after_low = over_x(4, lambda c: after.at[low(c)], lambda c: from_before.at[low(c)], place.x_next)
+    before_high = over_x(5, lambda c: before.at[high(c)], lambda c: from_after.at[high(c)], place.x_before)
+
+    for c in (0, 1):
+        hop_a[c].start()
+        hop_b[c].start()
+    for c in steps:
+        core_own[c].start()
+
+    turn = [Gather(place, ref, z_send.at[i], z_recv.at[i]) for i, ref in enumerate((transfer, inward, corner))]
     c_high, c_low = split(coupling[...])
     t_high, t_low = split(coupling_t[...])
     value = beside(g_rl)
@@ -182,66 +212,121 @@
     turn[1].start()
     corner[z] = beside(g_ll).astype(f32)
     turn[2].start()
-    for item in turn:
-        item.forward()
+
+    def pass_on(c):
+        hop_a[c].wait_recv()
+        end_a[c].start()
+        hop_b[c].wait_recv()
+        end_b[c].start()
+        if c + 2 < CHUNKS:
+            hop_a[c + 2].start()
+            hop_b[c + 2].start()
+
+    def weigh(c):
+        end_a[c].wait_recv()
+        end_b[c].wait_recv()
+        core_more[c].start()
+        core_own[c].wait_recv()
+        core_more[c].wait_recv()
+        rows = full(c)
+        pieces = [previous[rows, :], others[0, rows, :], others[1, rows, :], others[2, rows, :]]
+
+        def weighted(target):
+            total = weights[4 * target] * pieces[0]
+            for source in (1, 2, 3):
+                total = total + weights[4 * target + source] * pieces[source]
+            return total
+
+        two_away[rows, :] = weighted(2)
+        two_low[c].start()
+        two_high[c].start()
+        after[rows, :] = weighted(1)
+        after_high[c].start()
+        before[rows, :] = weighted(3)
+        before_low[c].start()
+        mine[rows, :] = weighted(0)
+
+    def add_passing(c):
+        two_low[c].wait_recv()
+        after[low(c), :] = after[low(c), :] + passing[0, c]
+        after_low[c].start()
+        two_high[c].wait_recv()
+        before[high(c), :] = before[high(c), :] + passing[1, c]
+        before_high[c].start()
+
+    def finish(c):
+        for item in (after_high, before_low, after_low, before_high):
+            item[c].wait_recv()
+        rows = full(c)
+        sigma[rows, :] = (mine[rows, :] + from_before[rows, :] + from_after[rows, :]).astype(bf16)
+
+    for t in range(CHUNKS + 3):
+        if t < CHUNKS:
+            pass_on(t)
+        if t < 3:
+            turn[t].forward()
+        if 0 <= t - 1 < CHUNKS:
+            weigh(t - 1)
+        if 0 <= t - 2 < CHUNKS:
+            add_passing(t - 2)
+        if 0 <= t - 3 < CHUNKS:
+            finish(t - 3)
     for item in turn:
         item.finish()
-
-    own[...] = jnp.zeros_like(own)
-
-    def step(index, _):
-        j = HALF - 1 - index
-
-        @pl.when(j == z)
-        def _():
-            own[...] = run[...]
-
-        run[...] = corner[j] + product(product(inward[j], run[...]), transfer[j])
-        return 0
-
-    cross = crossing(place, run, incoming, cross_send, cross_recv)
-
-    @pl.when(half == 1)
-    def _():
-        run[...] = corner[HALF - 1]
-
-    @pl.when(half == 0)
-    def _():
-        cross.wait_recv()
-        run[...] = incoming[...]
-
-    lax.fori_loop(half, jnp.where(half == 1, HALF, HALF - 1 - z), step, 0)
-
-    @pl.when(half == 1)
-    def _():
-        cross.start()
-        cross.wait_send()
-
-    @pl.when(half == 0)
-    def _():
-        own[...] = run[...]
-
-    value = own[...]
-    outer = real_right(value, coupling_t[...])
-    through[...] = product(inward[z], outer)
-    far[...] = real_left(coupling[...], outer).astype(bf16)
+    for group in (
+        hop_a, end_a, hop_b, end_b, core_own, core_more,
+        two_low, two_high, after_high, before_low, after_low, before_high,
+    ):
+        for item in group:
+            item.wait_send()
 
 
 def sweep_kernel(
-    transfer, inward, through, coupling, coupling_t, g_ll, g_rl, outer_rr, outer_rl, outer_ll,
-    state, far,
-    source, driven, run, own, incoming, send, recv, cross_send, cross_recv,
+    transfer, inward, corner, coupling, coupling_t, g_ll, g_rl, outer_rr, outer_rl, outer_ll,
+    state, retarded_far, lesser_far,
+    source, driven, run, own, kept, through, incoming, send, recv, cross_send, cross_recv,
 ):
     place = Place()
     z, half = place.z, place.half
-    enter(place)
+    enter([place.left, place.right, place.across])
+
+    def crossing(index, ref):
+        return sending(ref, incoming.at[index], cross_send.at[index], cross_recv.at[index], place.across)
+
+    over = crossing(0, kept)
+    up = crossing(1, run)
+    down = crossing(2, run)
+
     turn = Gather(place, source, send.at[0], recv.at[0])
     source[z] = real_left(coupling_t[...], real_right(beside(outer_rr), coupling[...]))
     turn.start()
     turn.forward()
+
+    own[...] = jnp.zeros_like(own)
+
+    def retarded_step(index, _):
+        j = HALF - 1 - index
+
+        @pl.when(j == z)
+        def _():
+            own[...] = kept[...]
+
+        kept[...] = corner[j] + product(product(inward[j], kept[...]), transfer[j])
+        return 0
+
+    def use_retarded():
+        outer = real_right(own[...], coupling_t[...])
+        through[...] = product(inward[z], outer)
+        retarded_far[...] = real_left(coupling[...], outer).astype(bf16)
+
+    @pl.when(half == 1)
+    def _():
+        kept[...] = corner[HALF - 1]
+        lax.fori_loop(1, HALF, retarded_step, 0)
+        over.start()
+        use_retarded()
+
     turn.finish()
-
-    own[...] = jnp.zeros_like(own)
 
     def forward_step(j, _):
         @pl.when(j == z)
@@ -252,32 +337,28 @@
         run[...] = product(product(factor, run[...]), factor, NT) + source[j]
         return 0
 
-    up = crossing(place, run, incoming, cross_send.at[0], cross_recv.at[0])
-
     @pl.when(half == 0)
     def _():
         run[...] = source[0]
+        lax.fori_loop(1, HALF, forward_step, 0)
+        up.start()
+        state[...] = own[...].astype(bf16)
+        over.wait_recv()
+        kept[...] = incoming[0]
+        lax.fori_loop(0, HALF - 1 - z, retarded_step, 0)
+        own[...] = kept[...]
+        use_retarded()
 
     @pl.when(half == 1)
     def _():
         up.wait_recv()
-        run[...] = incoming[...]
-
-    lax.fori_loop(1 - half, jnp.where(half == 0, HALF, z), forward_step, 0)
-
-    @pl.when(half == 0)
-    def _():
-        up.start()
-
-    @pl.when(half == 1)
-    def _():
-        own[...] = run[...]
-
-    value = own[...]
-    state[...] = value.astype(bf16)
+        run[...] = incoming[1]
+        lax.fori_loop(0, z, forward_step, 0)
+        state[...] = run[...].astype(bf16)
+
     left = beside(g_ll)
-    tail = exact_right(value, left, NT)
-    right = exact_left(jnp.concatenate([left, beside(g_rl)], axis=0), tail)
+    coupled = dot(jnp.concatenate([left, beside(g_rl)], axis=0), doubled(state[...])).astype(bf16)
+    right = dot(coupled, doubled(left), NT)
     mixed = product(through[...], beside(outer_rl) + right[BW:])
     turn = Gather(place, driven, send.at[1], recv.at[1])
     driven[z] = beside(outer_ll) + right[:BW] + mixed + adjoint(mixed)
@@ -302,31 +383,24 @@
         run[...] = product(product(factor, run[...]), factor, NT) + driven[j]
         return 0
 
-    down = crossing(place, run, incoming, cross_send.at[1], cross_recv.at[1])
-
     @pl.when(half == 1)
     def _():
         run[...] = driven[HALF - 1]
+        lax.fori_loop(1, HALF, backward_step, 0)
+        down.start()
 
     @pl.when(half == 0)
     def _():
         down.wait_recv()
-        run[...] = incoming[...]
-
-    lax.fori_loop(half, jnp.where(half == 1, HALF, HALF - 1 - z), backward_step, 0)
+        run[...] = incoming[2]
+        lax.fori_loop(0, HALF - 1 - z, backward_step, 0)
+        own[...] = run[...]
+
+    lesser_far[...] = real_left(coupling[...], real_right(own[...], coupling_t[...])).astype(bf16)
 
     @pl.when(half == 1)
     def _():
-        down.start()
-
-    @pl.when(half == 0)
-    def _():
-        own[...] = run[...]
-
-    far[...] = real_left(coupling[...], real_right(own[...], coupling_t[...])).astype(bf16)
-
-    @pl.when(half == 1)
-    def _():
+        over.wait_send()
         down.wait_send()
 
 
@@ -439,44 +513,59 @@
 WIDE = (BW, 2 * BW)
 
 
-def early(g_rl, g_lr, g_ll, coupling, coupling_t):
+def phonon(weights, previous, *operands):
+    stacked = pltpu.VMEM((STACKED, BLK), f32)
+    dma = pltpu.SemaphoreType.DMA
     return pl.pallas_call(
-        early_kernel,
-        out_shape=[shape((HALF,) + WIDE), shape((HALF,) + WIDE), shape(WIDE), shape(WIDE, bf16)],
-        in_specs=whole(5),
+        phonon_kernel,
+        out_shape=[shape((STACKED, BLK), bf16)] + [shape((HALF,) + WIDE)] * 3,
+        in_specs=[pl.BlockSpec(memory_space=pltpu.SMEM)] + whole(1 + len(operands)),
         out_specs=whole(4),
         scratch_shapes=[
-            pltpu.VMEM((HALF,) + WIDE, f32),
-            pltpu.VMEM(WIDE, f32),
-            pltpu.VMEM(WIDE, f32),
-            pltpu.VMEM(WIDE, f32),
-            pltpu.SemaphoreType.DMA((3, 6)),
-            pltpu.SemaphoreType.DMA((3, 6)),
-            pltpu.SemaphoreType.DMA,
-            pltpu.SemaphoreType.DMA,
+            pltpu.VMEM((3, STACKED, BLK), f32),
+            pltpu.VMEM((2, CHUNKS, PART, BLK), f32),
+            stacked,
+            stacked,
+            stacked,
+            pltpu.VMEM((2, CHUNKS, PART, BLK), f32),
+            stacked,
+            stacked,
+            stacked,
+            dma((3, 6)),
+            dma((3, 6)),
+            dma((4, CHUNKS)),
+            dma((4, CHUNKS)),
+            dma((2, CHUNKS)),
+            dma((2, CHUNKS)),
+            dma((6, CHUNKS)),
+            dma((6, CHUNKS)),
         ],
         compiler_params=pltpu.CompilerParams(
             collective_id=0, has_side_effects=True, vmem_limit_bytes=VMEM_LIMIT
         ),
-    )(g_rl, g_lr, g_ll, coupling, coupling_t)
+    )(weights, previous, *operands)
 
 
 def sweep(*operands):
+    wide = pltpu.VMEM(WIDE, f32)
+    dma = pltpu.SemaphoreType.DMA
     return pl.pallas_call(
         sweep_kernel,
-        out_shape=[shape(WIDE, bf16), shape(WIDE, bf16)],
+        out_shape=[shape(WIDE, bf16)] * 3,
         in_specs=whole(len(operands)),
-        out_specs=whole(2),
+        out_specs=whole(3),
         scratch_shapes=[
             pltpu.VMEM((HALF,) + WIDE, f32),
             pltpu.VMEM((HALF,) + WIDE, f32),
-            pltpu.VMEM(WIDE, f32),
-            pltpu.VMEM(WIDE, f32),
-            pltpu.VMEM(WIDE, f32),
-            pltpu.SemaphoreType.DMA((2, 6)),
-            pltpu.SemaphoreType.DMA((2, 6)),
-            pltpu.SemaphoreType.DMA((2,)),
-            pltpu.SemaphoreType.DMA((2,)),
+            wide,
+            wide,
+            wide,
+            wide,
+            pltpu.VMEM((3,) + WIDE, f32),
+            dma((2, 6)),
+            dma((2, 6)),
+            dma((3,)),
+            dma((3,)),
         ],
         compiler_params=pltpu.CompilerParams(
             collective_id=1, has_side_effects=True, vmem_limit_bytes=VMEM_LIMIT
@@ -532,28 +621,28 @@
     return jnp.sum(emission + absorption, axis=-1)
 
 
-def slab_work(green, sigma, coupling):
-    lead, tail = slice(0, BW), slice(SLAB_ORBITALS - BW, SLAB_ORBITALS)
-    g_ll, g_rl, g_lr = green[:, lead, lead], green[:, tail, lead], green[:, lead, tail]
-    coupling_t = coupling.T
-    transfer, inward, through, retarded_far = early(g_rl, g_lr, g_ll, coupling, coupling_t)
-    outer_right, outer_left, outer_blocks = local_terms(green, sigma)
-    state, lesser_far = sweep(
-        transfer, inward, through, coupling, coupling_t, g_ll, g_rl,
-        outer_right[PAIRS - 1], outer_right[0], outer_left,
-    )
-    return final_terms(green, state, retarded_far, lesser_far, outer_right, outer_blocks)
-
-
 def body(green_ret, prev_lesser, coupling_index, coupling_values, phonon_shift, phonon_weight):
     green = green_ret[0, 0]
     coupling = dense_coupling(coupling_index[0], coupling_values[0])
-    my_energy = lax.axis_index("energy")
-    received = lax.all_gather(prev_lesser[0, 0], "energy", axis=0, tiled=False)
-    sources = jnp.arange(received.shape[0], dtype=jnp.int32)
-    weights = partner_weights(my_energy, sources, phonon_shift, phonon_weight)
-    sigma = sum(weights[f] * received[f] for f in range(received.shape[0])).astype(bf16)
-    retarded, lesser = slab_work(green, sigma, coupling)
+    coupling_t = coupling.T
+    lead, tail = slice(0, BW), slice(SLAB_ORBITALS - BW, SLAB_ORBITALS)
+    g_ll, g_rl, g_lr = green[:, lead, lead], green[:, tail, lead], green[:, lead, tail]
+
+    energy = lax.axis_index("energy")
+    flipped = energy + 2 - 4 * (energy // 2 % 2)
+    sources = jnp.stack([energy, energy ^ 1, flipped, flipped ^ 1]).astype(jnp.int32)
+    targets = (energy + 4 * jnp.arange(4, dtype=jnp.int32)) % 16
+    weights = partner_weights(targets[:, None], sources[None, :], phonon_shift, phonon_weight).reshape(16)
+
+    sigma, transfer, inward, corner = phonon(
+        weights, prev_lesser.reshape(STACKED, BLK), g_rl, g_lr, g_ll, coupling, coupling_t
+    )
+    outer_right, outer_left, outer_blocks = local_terms(green, sigma.reshape(2, SLAB_ORBITALS, BLK))
+    state, retarded_far, lesser_far = sweep(
+        transfer, inward, corner, coupling, coupling_t, g_ll, g_rl,
+        outer_right[PAIRS - 1], outer_right[0], outer_left,
+    )
+    retarded, lesser = final_terms(green, state, retarded_far, lesser_far, outer_right, outer_blocks)
     return retarded[None, None], lesser[None, None]
 
 

time: 323 us -> 221 us (0.68)
  waiting for transfers between devices: 58.4 us -> 0 us
  other arithmetic: 20.4 us -> 0.9 us
  between operations: 14.2 us -> 0.72 us
  Pallas kernels: 222 us -> 210 us
    all_gather x1 -> x0, waiting for transfers between devices: 57.7 us -> none  [body(): received = lax.all_gather(prev_lesser[0, 0], 'energy', axis=0, tiled=False)]
    convert_element_type x1 -> x0, other arithmetic: 20.3 us -> none  [body(): sum((weights[f] * received[f] for f in range(received.shape[0])))]
    pallas_call x2, Pallas kernels: 186 us -> 174 us  [the longest x1 88.7 us: phonon(): pl.pallas_call(phonon_kernel, out_shape=[shape((STACKED, BLK), bf16)] + [...]
  transfers between devices with their start and end apart: 1 -> 0, of which waited for: 1 -> 0; matrix products, arithmetic and copies ran while one was open for 1% -> 0% of each run, Pallas kernels for 28% -> 0%
where the time goes in v2:
time: 221 us
  Pallas kernels  210 us (95%)
  local copies, waits for them, and re-layouts  7.39 us (3%)
    pallas_call x1, Pallas kernels, phonon(): pl.pallas_call(phonon_kernel, out_shape=[shape((STACKED, BLK), bf16)] + [...  88.7 us
    pallas_call x1, Pallas kernels, sweep(): pl.pallas_call(sweep_kernel, out_shape=[shape(WIDE, bf16)] * 3, in_specs=...  85 us
    pallas_call x1, Pallas kernels, local_terms(): pl.pallas_call(local_kernel, out_shape=[shape((PAIRS, 2, BW, BW)), shape(...  21.7 us
    pallas_call x1, Pallas kernels, final_terms(): pl.pallas_call(final_kernel, out_shape=[shape((2, SLAB_ORBITALS, BLK)), s...  14.9 us

profile of v2, /device:TPU:0, one launch (start us, length us, event | category | flops | bytes accessed | tf_op | source)
XLA Modules:
  0.0 221.1 jit_solution(12687466995025128430)
XLA Ops:
  0.7 0.1 pad_add_fusion
  0.8 0.8 slice_bitcast_fusion.3
  1.5 0.8 slice_bitcast_fusion.5
  2.3 0.7 broadcast_add_fusion
  3.0 0.1 add_reduce_fusion
  3.1 0.6 reshape.85.weights
  3.7 1.7 convolution_bitcast_fusion
  5.4 0.2 copy.13
  5.6 0.0 copy-start
  5.6 0.8 copy.14.coupling
  6.5 2.0 fusion.8
  8.5 0.0 copy-done
  8.5 88.7 %shard_map.77 = (bf16[3072,128]{1,0:T(8,128)(2,1)}, f32[4,256,512]{2,1,0:T(8,128)}, f32[4,256,512]{2,1,0:T(8,128)}, f32[4,256,512]{2,1,0:T(8,128)}) custom-call(f32[16]{0:T(128)} %reshape.85.weights, f32[3072,128]{1,0:T(8,128)} %bitcast.51, bf16[2,256,256]{2,1,0:T(8,128)(2,1)} %get-tuple-element.28.g_rl, bf16[2,256,256]{2,1,0:T(8,128)(2,1)} %get-tuple-element.27.g_lr, ...), custom_call_target="tpu_custom_call" | custom-call | tf_op jit(solution)/shard_map/pallas_call | solution.py:519
  97.2 21.7 %shard_map.78 = (f32[6,2,256,256]{3,2,1,0:T(8,128)}, f32[2,256,256]{2,1,0:T(8,128)}, f32[2,1536,128]{2,1,0:T(8,128)}) custom-call(bf16[2,1536,1536]{2,1,0:T(8,128)(2,1)} %bitcast.46, bf16[2,1536,128]{2,1,0:T(8,128)(2,1)} %bitcast.53), custom_call_target="tpu_custom_call" | custom-call | tf_op jit(solution)/shard_map/pallas_call | solution.py:577
  118.9 2.2 %slice_bitcast_fusion = (f32[2,256,256]{2,1,0:T(8,128)}, f32[2,256,256]{2,1,0:T(8,128)}) fusion(f32[6,2,256,256]{3,2,1,0:T(8,128)} %get-tuple-element.18.outer_right), kind=kLoop, calls=%fused_computation.1 | loop fusion | bytes 2097152 | tf_op jit(solution)/shard_map/squeeze | solution.py:643
  121.2 85.0 %shard_map.79 = (bf16[256,512]{1,0:T(8,128)(2,1)}, bf16[256,512]{1,0:T(8,128)(2,1)}, bf16[256,512]{1,0:T(8,128)(2,1)}) custom-call(f32[4,256,512]{2,1,0:T(8,128)} %get-tuple-element.14.transfer, f32[4,256,512]{2,1,0:T(8,128)} %get-tuple-element.15.inward, f32[4,256,512]{2,1,0:T(8,128)} %get-tuple-element.16.corner, f32[256,256]{1,0:T(8,128)} %copy.14.coupling, ...), custom_call_target="tpu_custom_call" | custom-call | tf_op jit(solution)/shard_map/pallas_call | solution.py:552
  206.2 14.9 %shard_map.80 = (f32[2,1536,128]{2,1,0:T(8,128)}, f32[2,1536,128]{2,1,0:T(8,128)}) custom-call(bf16[2,1536,1536]{2,1,0:T(8,128)(2,1)} %bitcast.47, bf16[256,512]{1,0:T(8,128)(2,1)} %get-tuple-element.20.state, bf16[256,512]{1,0:T(8,128)(2,1)} %get-tuple-element.21.retarded_far, bf16[256,512]{1,0:T(8,128)(2,1)} %get-tuple-element.22.lesser_far, ...), custom_call_target="tpu_custom_call" | custom-call | tf_op jit(solution)/shard_map/pallas_call | solution.py:592
  (3 shorter events, 0.0 us)
Async XLA Ops:
  5.6 2.9 %copy-start = (f32[32,8,2,128]{3,1,2,0:T(8,128)}, f32[32,8,2,128]{3,1,2,0:T(8,128)S(1)}, u32[]{:S(2)}) copy-start(f32[32,8,2,128]{3,1,2,0:T(8,128)S(1)} %copy.25) | copy-start | bytes 786436

commit v3 on v2

v3 whole, which is shorter than its diff:
```python
import functools

import jax
import jax.numpy as jnp
from jax import lax
from jax.experimental import pallas as pl
from jax.experimental.pallas import tpu as pltpu
from jax.sharding import PartitionSpec as P

SLAB_ORBITALS = 1536
BW = 256
BLK = 128
NBLK = 12
NBW = 2
PAIRS = SLAB_ORBITALS // BW
HALF = 4

FULL_PRECISION = lax.Precision.HIGHEST
MESH = pl.DeviceIdType.MESH
VMEM_LIMIT = 58 * 1024 * 1024
NN = (((1,), (0,)), ((), ()))
NT = (((1,), (1,)), ((), ()))

f32 = jnp.float32
bf16 = jnp.bfloat16


def dot(left, right, dims=NN):
    return lax.dot_general(left, right, dims, preferred_element_type=f32)


def split(value):
    high = value.astype(bf16)
    return high, (value - high.astype(f32)).astype(bf16)


def turned(value):
    width = value.shape[1] // 2
    return jnp.concatenate([-value[:, width:], value[:, :width]], axis=1)


def doubled(value):
    return jnp.concatenate([value, turned(value)], axis=0)


def product(left, right, dims=NN):
    left_high, left_low = split(left)
    right_high, right_low = split(right)
    main = doubled(right_high)
    return (
        dot(left_high, main, dims) + dot(left_low, main, dims) + dot(left_high, doubled(right_low), dims)
    )


def real_left(matrix, value):
    matrix_high, matrix_low = split(matrix)
    value_high, value_low = split(value)
    return dot(matrix_high, value_high) + dot(matrix_high, value_low) + dot(matrix_low, value_high)


def real_right(value, matrix):
    matrix_high, matrix_low = split(matrix)
    parts = []
    for part in (value[:, :BW], value[:, BW:]):
        high, low = split(part)
        parts.append(dot(high, matrix_high) + dot(low, matrix_high) + dot(high, matrix_low))
    return jnp.concatenate(parts, axis=1)


def beside(ref):
    return jnp.concatenate([ref[0], ref[1]], axis=1)


def adjoint(value):
    return jnp.concatenate([value[:, :BW].T, -value[:, BW:].T], axis=1)


class Place:
    def __init__(self):
        slab, energy = lax.axis_index("slab"), lax.axis_index("energy")
        self.half = slab // HALF
        self.z = slab % HALF
        base = self.half * HALF
        self.right = {"slab": base + (self.z + 1) % HALF}
        self.left = {"slab": base + (self.z + HALF - 1) % HALF}
        self.away = [{"slab": base + (self.z + d) % HALF} for d in (1, 2, 3)]
        other_half = (slab + HALF) % (2 * HALF)
        flipped = energy + 2 - 4 * (energy // 2 % 2)
        self.across = {"slab": other_half}
        self.across_flipped = {"slab": other_half, "energy": flipped}
        self.core = {"energy": energy + 1 - 2 * (energy % 2)}
        self.x_next = {"energy": (energy + 4) % 16}
        self.x_before = {"energy": (energy + 12) % 16}


def enter(others):
    barrier = pltpu.get_barrier_semaphore()
    for other in others:
        pl.semaphore_signal(barrier, inc=1, device_id=other, device_id_type=MESH)
    pl.semaphore_wait(barrier, len(others))


def sending(source, target, send, recv, device):
    return pltpu.make_async_remote_copy(
        src_ref=source, dst_ref=target, send_sem=send, recv_sem=recv, device_id=device, device_id_type=MESH
    )


class Gather:
    def __init__(self, place, slots, send, recv):
        z = place.z
        low, high = pl.ds(0, BW // 2), pl.ds(BW // 2, BW // 2)
        before, after, opposite = (z + 3) % HALF, (z + 1) % HALF, (z + 2) % HALF

        def copy(index, slot, rows, target):
            part = slots.at[slot, rows]
            return sending(part, part, send.at[index], recv.at[index], target)

        self.first = [
            copy(0, z, low, place.right),
            copy(1, z, high, place.left),
            copy(2, z, high, place.right),
            copy(3, z, low, place.left),
        ]
        self.arrive = [
            copy(0, before, low, place.right),
            copy(1, after, high, place.left),
            copy(2, before, high, place.right),
            copy(3, after, low, place.left),
        ]
        self.relay = [copy(4, before, low, place.right), copy(5, after, high, place.left)]
        self.last = [copy(4, opposite, low, place.right), copy(5, opposite, high, place.left)]

    def start(self):
        for item in self.first:
            item.start()

    def forward(self):
        for index in (0, 1):
            self.arrive[index].wait_recv()
            self.relay[index].start()

    def finish(self):
        for item in self.arrive[2:] + self.last:
            item.wait_recv()
        for item in self.first + self.relay:
            item.wait_send()


CHUNKS = 6
ROWS = SLAB_ORBITALS // CHUNKS
QUARTER = BW // HALF


def unit():
    row = lax.broadcasted_iota(jnp.int32, WIDE, 0)
    column = lax.broadcasted_iota(jnp.int32, WIDE, 1)
    return (row == column).astype(f32)


def phonon_kernel(
    weights, previous, g_rl, g_lr, g_ll, coupling, coupling_t,
    sigma, transfer, inward, corner, retarded, reach,
    others, relay, two_away, after, before, passing, from_before, from_after, mine,
    run, incoming,
    z_send, z_recv, y_send, y_recv, core_send, core_recv, x_send, x_recv, cross_send, cross_recv,
):
    place = Place()
    enter([place.left, place.right, place.across, place.across_flipped, place.core, place.x_next, place.x_before])
    z, half = place.z, place.half
    steps = range(CHUNKS)

    def rows(c):
        return pl.ds(c * ROWS, ROWS)

    def part(ref, index):
        return lambda c: ref.at[index, rows(c)]

    def both(ref):
        return lambda c: ref.at[:, rows(c)]

    def copies(sems, kind, source, target, device):
        send, recv = sems
        return [sending(source(c), target(c), send.at[kind, c], recv.at[kind, c], device) for c in steps]

    y, core, x = (y_send, y_recv), (core_send, core_recv), (x_send, x_recv)
    hop_a = copies(y, 0, part(previous, 0), part(relay, 0), place.across)
    end_a = copies(y, 1, part(relay, 0), part(others.at[1], 0), place.across_flipped)
    hop_b = copies(y, 2, part(previous, 1), part(relay, 1), place.across_flipped)
    end_b = copies(y, 3, part(relay, 1), part(others.at[1], 1), place.across)
    core_own = copies(core, 0, both(previous), both(others.at[0]), place.core)
    core_more = copies(core, 1, both(others.at[1]), both(others.at[2]), place.core)
    two_low = copies(x, 0, part(two_away, 0), part(passing, 0), place.x_next)
    two_high = copies(x, 1, part(two_away, 1), part(passing, 1), place.x_before)
    after_high = copies(x, 2, part(after, 1), part(from_before, 1), place.x_next)
    before_low = copies(x, 3, part(before, 0), part(from_after, 0), place.x_before)
    after_low = copies(x, 4, part(after, 0), part(from_before, 0), place.x_next)
    before_high = copies(x, 5, part(before, 1), part(from_after, 1), place.x_before)

    for c in (0, 1):
        hop_a[c].start()
        hop_b[c].start()
    for c in steps:
        core_own[c].start()

    turn = [Gather(place, ref, z_send.at[i], z_recv.at[i]) for i, ref in enumerate((transfer, inward, corner))]
    c_high, c_low = split(coupling[...])
    t_high, t_low = split(coupling_t[...])
    value = beside(g_rl)
    transfer[z] = dot(t_high, value) + dot(t_low, value)
    turn[0].start()
    parts = [dot(g_lr[i], c_high) + dot(g_lr[i], c_low) for i in (0, 1)]
    inward[z] = jnp.concatenate(parts, axis=1)
    corner[z] = beside(g_ll).astype(f32)

    def pass_on(c):
        hop_a[c].wait_recv()
        end_a[c].start()
        hop_b[c].wait_recv()
        end_b[c].start()
        if c + 2 < CHUNKS:
            hop_a[c + 2].start()
            hop_b[c + 2].start()

    def weigh(c):
        end_a[c].wait_recv()
        end_b[c].wait_recv()
        core_more[c].start()
        core_own[c].wait_recv()
        core_more[c].wait_recv()
        pieces = [previous[:, rows(c)]] + [others[i, :, rows(c)] for i in (0, 1, 2)]

        def weighted(target):
            total = weights[4 * target] * pieces[0]
            for source in (1, 2, 3):
                total = total + weights[4 * target + source] * pieces[source]
            return total

        two_away[:, rows(c)] = weighted(2)
        two_low[c].start()
        two_high[c].start()
        after[:, rows(c)] = weighted(1)
        after_high[c].start()
        before[:, rows(c)] = weighted(3)
        before_low[c].start()
        mine[:, rows(c)] = weighted(0)

    def add_passing(c):
        two_low[c].wait_recv()
        after[0, rows(c)] = after[0, rows(c)] + passing[0, rows(c)]
        after_low[c].start()
        two_high[c].wait_recv()
        before[1, rows(c)] = before[1, rows(c)] + passing[1, rows(c)]
        before_high[c].start()

    def finish(c):
        for item in (after_high, before_low, after_low, before_high):
            item[c].wait_recv()
        sigma[:, rows(c)] = (mine[:, rows(c)] + from_before[:, rows(c)] + from_after[:, rows(c)]).astype(bf16)

    over = sending(run, incoming, cross_send, cross_recv, place.across)

    def retarded_step(index, _):
        j = HALF - 1 - index

        @pl.when(j == z)
        def _():
            retarded[...] = run[...]

        run[...] = corner[j] + product(product(inward[j], run[...]), transfer[j])
        return 0

    def upper_corners():
        reach[...] = unit()

        @pl.when(half == 1)
        def _():
            retarded[...] = jnp.zeros_like(retarded)
            run[...] = corner[HALF - 1]
            lax.fori_loop(1, HALF, retarded_step, 0)
            over.start()

            def step(index, _):
                reach[...] = product(inward[z - 1 - index], reach[...])
                return 0

            lax.fori_loop(0, z, step, 0)

        @pl.when(half == 0)
        def _():
            def step(j, _):
                reach[...] = product(transfer[j], reach[...])
                return 0

            lax.fori_loop(z + 1, HALF, step, 0)

    for t in range(CHUNKS + 3):
        if t < CHUNKS:
            pass_on(t)
        if 0 <= t - 1 < CHUNKS:
            weigh(t - 1)
        if t in (1, 3, 5):
            turn[t // 2].forward()
            if t < 5:
                turn[t // 2 + 1].start()
        if 0 <= t - 2 < CHUNKS:
            add_passing(t - 2)
        if 0 <= t - 3 < CHUNKS:
            finish(t - 3)
        if t == CHUNKS + 1:
            for item in turn:
                item.finish()
            upper_corners()

    @pl.when(half == 0)
    def _():
        over.wait_recv()
        retarded[...] = incoming[...]

    @pl.when(half == 1)
    def _():
        over.wait_send()

    for group in (
        hop_a, end_a, hop_b, end_b, core_own, core_more,
        two_low, two_high, after_high, before_low, after_low, before_high,
    ):
        for item in group:
            item.wait_send()


class Shipment:
    def __init__(self, place, term, parts, quarter, total, send, recv):
        z = place.z

        def rows(index):
            return pl.ds(pl.multiple_of((index % HALF) * QUARTER, QUARTER), QUARTER)

        self.term, self.parts, self.quarter, self.here = term, parts, quarter, rows(z)
        self.spread = [
            sending(term.at[rows(z + d)], parts.at[d - 1], send.at[d - 1], recv.at[d - 1], place.away[d - 1])
            for d in (1, 2, 3)
        ]
        self.cross = sending(quarter, total.at[rows(z)], send.at[3], recv.at[3], place.across)
        self.hand = [
            sending(total.at[rows(z)], total.at[rows(z)], send.at[3 + d], recv.at[3 + d], place.away[d - 1])
            for d in (1, 2, 3)
        ]
        self.get = [
            sending(total.at[rows(z - d)], total.at[rows(z - d)], send.at[3 + d], recv.at[3 + d], place.away[d - 1])
            for d in (1, 2, 3)
        ]

    def start(self):
        for item in self.spread:
            item.start()

    def pass_over(self):
        for item in self.spread:
            item.wait_recv()
        self.quarter[...] = self.term[self.here, :] + self.parts[0] + self.parts[1] + self.parts[2]
        self.cross.start()

    def hand_on(self):
        self.cross.wait_recv()
        for item in self.hand:
            item.start()

    def arrive(self):
        for item in self.get:
            item.wait_recv()

    def sent(self):
        for item in self.spread + [self.cross]:
            item.wait_send()

    def handed(self):
        for item in self.hand:
            item.wait_send()


def sweep_kernel(
    transfer, inward, corner, retarded, reach, coupling, coupling_t, g_ll, g_rl, outer_rr, outer_rl, outer_ll,
    green_hbm, outer_right, outer_blocks,
    lesser_far, retarded_part, lesser_part,
    green, source, driven, own, through, term, parts, quarter, total, coupled, weighted,
    send, recv, ship_send, ship_recv, load,
):
    place = Place()
    z, half = place.z, place.half
    fetch = pltpu.make_async_copy(green_hbm, green, load)
    fetch.start()
    enter(place.away + [place.across])
    ship = Shipment(place, term, parts, quarter, total, ship_send, ship_recv)
    left, last = pl.ds(0, BW), pl.ds(SLAB_ORBITALS - BW, BW)
    stripe = 512

    def congruence(factor, value):
        return product(product(factor, value), factor, NT)

    turn = Gather(place, source, send.at[0], recv.at[0])
    source[z] = real_left(coupling_t[...], real_right(beside(outer_rr), coupling[...]))

    @pl.when(half == 0)
    def _():
        term[...] = congruence(reach[...], source[z])
        ship.start()

    turn.start()

    @pl.when(half == 0)
    def _():
        ship.pass_over()

    turn.forward()

    own[...] = retarded[...]

    def retarded_step(index, _):
        j = HALF - 1 - index
        own[...] = corner[j] + product(product(inward[j], own[...]), transfer[j])
        return 0

    @pl.when(half == 0)
    def _():
        lax.fori_loop(0, HALF - 1 - z, retarded_step, 0)

    def use_retarded():
        outer = real_right(own[...], coupling_t[...])
        through[...] = product(inward[z], outer)
        factor = doubled(real_left(coupling[...], outer).astype(bf16))
        fetch.wait()
        for start in range(0, SLAB_ORBITALS, stripe):
            span = pl.ds(start, stripe)
            piece = jnp.concatenate([green[0, span, last], green[1, span, last]], axis=1)
            weighted[span, :] = dot(piece, factor).astype(bf16)

        def pair(m, _):
            span = pl.ds(pl.multiple_of(m * BW, BW), BW)
            result = dot(
                weighted[span, :], doubled(jnp.concatenate([green[0, last, span], green[1, last, span]], axis=1))
            )
            for k in (0, 1):
                block = pl.ds(pl.multiple_of(m * BW + k * BLK, BLK), BLK)
                here = slice(k * BLK, (k + 1) * BLK)
                for i in (0, 1):
                    there = slice(i * BW + k * BLK, i * BW + (k + 1) * BLK)
                    retarded_part[i, block, :] = green[i, block, block].astype(f32) + result[here, there]
            return 0

        lax.fori_loop(0, PAIRS, pair, 0)

    use_retarded()

    @pl.when(half == 1)
    def _():
        ship.hand_on()

    turn.finish()
    own[...] = jnp.zeros_like(own)

    def forward_step(j, _):
        own[...] = congruence(transfer[j], own[...]) + source[j]
        return 0

    @pl.when(half == 0)
    def _():
        @pl.when(z > 0)
        def _():
            own[...] = source[0]

        lax.fori_loop(1, z, forward_step, 0)

    @pl.when(half == 1)
    def _():
        ship.arrive()
        own[...] = total[...]
        lax.fori_loop(0, z, forward_step, 0)

    state = doubled(own[...].astype(bf16))
    corner_l = beside(g_ll)
    near = dot(jnp.concatenate([corner_l, beside(g_rl)], axis=0), state).astype(bf16)
    right = dot(near, doubled(corner_l), NT)
    mixed = product(through[...], beside(outer_rl) + right[BW:])
    turn = Gather(place, driven, send.at[1], recv.at[1])
    driven[z] = beside(outer_ll) + right[:BW] + mixed + adjoint(mixed)

    @pl.when(half == 1)
    def _():
        term[...] = congruence(reach[...], driven[z])
        ship.start()

    turn.start()

    @pl.when(half == 1)
    def _():
        ship.pass_over()

    turn.forward()

    for start in range(0, SLAB_ORBITALS, stripe):
        span = pl.ds(start, stripe)
        piece = jnp.concatenate([green[0, span, left], green[1, span, left]], axis=1)
        result = dot(piece, state).astype(bf16)
        coupled[0, span, :] = result[:, :BW]
        coupled[1, span, :] = result[:, BW:]
        coupled[2, span, :] = -result[:, :BW]

    def against(left_rows, right_rows):
        first = coupled[0:2, left_rows, :].reshape(2 * BW, BW)
        second = coupled[1:3, left_rows, :].reshape(2 * BW, BW)
        result = dot(first, green[0, right_rows, left], NT) + dot(second, green[1, right_rows, left], NT)
        return result.reshape(2, BW, BW)

    def pair(m, _):
        span = pl.ds(pl.multiple_of(m * BW, BW), BW)
        far_right = (outer_right[m] + against(last, span)).astype(bf16)
        mixed = dot(weighted[span, :], doubled(jnp.concatenate([far_right[0], far_right[1]], axis=1)))
        local = against(span, span)
        for k in (0, 1):
            block = pl.ds(pl.multiple_of(m * BW + k * BLK, BLK), BLK)
            here = slice(k * BLK, (k + 1) * BLK)
            for i in (0, 1):
                there = slice(i * BW + k * BLK, i * BW + (k + 1) * BLK)
                mix = mixed[here, there]
                mirrored = mix.T if i == 0 else -mix.T
                lesser_part[i, block, :] = outer_blocks[i, block, :] + local[i, here, here] + mix + mirrored
        return 0

    lax.fori_loop(0, PAIRS, pair, 0)

    @pl.when(half == 0)
    def _():
        ship.hand_on()

    turn.finish()
    own[...] = jnp.zeros_like(own)

    def backward_step(index, _):
        j = HALF - 1 - index
        own[...] = congruence(inward[j], own[...]) + driven[j]
        return 0

    @pl.when(half == 1)
    def _():
        @pl.when(z < HALF - 1)
        def _():
            own[...] = driven[HALF - 1]

        lax.fori_loop(1, HALF - 1 - z, backward_step, 0)

    @pl.when(half == 0)
    def _():
        ship.arrive()
        own[...] = total[...]
        lax.fori_loop(0, HALF - 1 - z, backward_step, 0)

    lesser_far[...] = real_left(coupling[...], real_right(own[...], coupling_t[...])).astype(bf16)
    ship.sent()
    ship.handed()


def local_kernel(green, sigma, outer_right, outer_rr, outer_rl, outer_left, outer_blocks, scaled):
    rows = 512

    def scale(n, _):
        columns = pl.ds(pl.multiple_of(n * BLK, BLK), BLK)
        real, imag = sigma[0, columns, :], sigma[1, columns, :]
        factor = jnp.concatenate(
            [jnp.concatenate([real, imag], axis=1), jnp.concatenate([-imag, real], axis=1)], axis=0
        )
        for start in range(0, SLAB_ORBITALS, rows):
            span = pl.ds(start, rows)
            piece = jnp.concatenate([green[0, span, columns], green[1, span, columns]], axis=1)
            result = dot(piece, factor).astype(bf16)
            scaled[0, span, columns] = result[:, :BLK]
            scaled[1, span, columns] = result[:, BLK:]
            scaled[2, span, columns] = -result[:, :BLK]
        return 0

    lax.fori_loop(0, NBLK, scale, 0)
    last = pl.ds(SLAB_ORBITALS - BW, BW)

    def against(left_rows, right_rows):
        first = scaled[0:2, left_rows, :].reshape(2 * BW, SLAB_ORBITALS)
        second = scaled[1:3, left_rows, :].reshape(2 * BW, SLAB_ORBITALS)
        total = dot(first, green[0, right_rows, :], NT) + dot(second, green[1, right_rows, :], NT)
        return total.reshape(2, BW, BW)

    def pair(m, _):
        span = pl.ds(pl.multiple_of(m * BW, BW), BW)
        far = against(last, span)
        outer_right[m] = far
        local = against(span, span)
        first = pl.ds(pl.multiple_of(m * BW, BW), BLK)
        second = pl.ds(pl.multiple_of(m * BW + BLK, BLK), BLK)
        outer_blocks[:, first, :] = local[:, :BLK, :BLK]
        outer_blocks[:, second, :] = local[:, BLK:, BLK:]

        @pl.when(m == 0)
        def _():
            outer_left[...] = local
            outer_rl[...] = far

        @pl.when(m == PAIRS - 1)
        def _():
            outer_rr[...] = far

        return 0

    lax.fori_loop(0, PAIRS, pair, 0)


def final_kernel(green, lesser_far, retarded_part, lesser_part, retarded_out, lesser_out):
    right = jnp.concatenate([green[0], green[1]], axis=1)
    weighted = dot(right, doubled(lesser_far[...])).astype(bf16)
    real, imag = weighted[:, :BW], weighted[:, BW:]
    first = jnp.concatenate([real, imag], axis=0)
    second = jnp.concatenate([imag, -real], axis=0)
    total = dot(first, green[0], NT) + dot(second, green[1], NT)
    retarded_out[...] = retarded_part[...]
    for k in (0, 1):
        block = slice(k * BLK, (k + 1) * BLK)
        for i in (0, 1):
            here = slice(i * BW + k * BLK, i * BW + (k + 1) * BLK)
            lesser_out[i, block, :] = lesser_part[i, block, :] + total[here, block]


def whole(count):
    return [pl.BlockSpec(memory_space=pltpu.VMEM)] * count


def shape(dims, dtype=f32):
    return jax.ShapeDtypeStruct(dims, dtype)


WIDE = (BW, 2 * BW)


def phonon(weights, previous, *operands):
    stacked = pltpu.VMEM((2, SLAB_ORBITALS, BLK), f32)
    dma = pltpu.SemaphoreType.DMA
    return pl.pallas_call(
        phonon_kernel,
        out_shape=[shape((2, SLAB_ORBITALS, BLK), bf16)] + [shape((HALF,) + WIDE)] * 3 + [shape(WIDE)] * 2,
        in_specs=[pl.BlockSpec(memory_space=pltpu.SMEM)] + whole(1 + len(operands)),
        out_specs=whole(6),
        scratch_shapes=[pltpu.VMEM((3, 2, SLAB_ORBITALS, BLK), f32)]
        + [stacked] * 8
        + [pltpu.VMEM(WIDE, f32)] * 2
        + [
            dma((3, 6)),
            dma((3, 6)),
            dma((4, CHUNKS)),
            dma((4, CHUNKS)),
            dma((2, CHUNKS)),
            dma((2, CHUNKS)),
            dma((6, CHUNKS)),
            dma((6, CHUNKS)),
            dma,
            dma,
        ],
        compiler_params=pltpu.CompilerParams(
            collective_id=0, has_side_effects=True, vmem_limit_bytes=VMEM_LIMIT
        ),
    )(weights, previous, *operands)


def sweep(green, *operands):
    wide = pltpu.VMEM(WIDE, f32)
    dma = pltpu.SemaphoreType.DMA
    specs = whole(len(operands) + 1)
    specs[12] = pl.BlockSpec(memory_space=pl.ANY)
    return pl.pallas_call(
        sweep_kernel,
        out_shape=[shape(WIDE, bf16)] + [shape((2, SLAB_ORBITALS, BLK))] * 2,
        in_specs=specs,
        out_specs=whole(3),
        scratch_shapes=[
            pltpu.VMEM((2, SLAB_ORBITALS, SLAB_ORBITALS), bf16),
            pltpu.VMEM((HALF,) + WIDE, f32),
            pltpu.VMEM((HALF,) + WIDE, f32),
            wide,
            wide,
            wide,
            pltpu.VMEM((3, QUARTER, 2 * BW), f32),
            pltpu.VMEM((QUARTER, 2 * BW), f32),
            wide,
            pltpu.VMEM((3, SLAB_ORBITALS, BW), bf16),
            pltpu.VMEM((SLAB_ORBITALS, 2 * BW), bf16),
            dma((2, 6)),
            dma((2, 6)),
            dma((7,)),
            dma((7,)),
            dma,
        ],
        compiler_params=pltpu.CompilerParams(
            collective_id=1, has_side_effects=True, vmem_limit_bytes=VMEM_LIMIT
        ),
    )(*operands[:12], green, *operands[12:])


def local_terms(green, sigma):
    return pl.pallas_call(
        local_kernel,
        out_shape=[
            shape((PAIRS, 2, BW, BW)),
            shape((2, BW, BW)),
            shape((2, BW, BW)),
            shape((2, BW, BW)),
            shape((2, SLAB_ORBITALS, BLK)),
        ],
        in_specs=whole(2),
        out_specs=whole(5),
        scratch_shapes=[pltpu.VMEM((3, SLAB_ORBITALS, SLAB_ORBITALS), bf16)],
        compiler_params=pltpu.CompilerParams(vmem_limit_bytes=VMEM_LIMIT),
    )(green, sigma)


def final_terms(*operands):
    strip = pl.BlockSpec((2, BW, BLK), lambda m: (0, m, 0))
    return pl.pallas_call(
        final_kernel,
        grid=(PAIRS,),
        out_shape=[shape((2, SLAB_ORBITALS, BLK))] * 2,
        in_specs=[
            pl.BlockSpec((2, BW, BW), lambda m: (0, m, PAIRS - 1)),
            pl.BlockSpec(WIDE, lambda m: (0, 0)),
            strip,
            strip,
        ],
        out_specs=[strip, strip],
        compiler_params=pltpu.CompilerParams(vmem_limit_bytes=VMEM_LIMIT),
    )(*operands)


def dense_coupling(block_index, block_values):
    positions = jnp.arange(NBW, dtype=jnp.int32)[None, :]
    row_select = (block_index[:, 0:1] == positions).astype(jnp.float32)
    column_select = (block_index[:, 1:2] == positions).astype(jnp.float32)
    dense = jnp.einsum(
        "br,bc,bij->ricj", row_select, column_select, block_values, precision=FULL_PRECISION
    )
    return dense.reshape(BW, BW)


def partner_weights(targets, sources, phonon_shift, phonon_weight):
    target_column = jnp.asarray(targets)[..., None]
    source_column = jnp.asarray(sources)[..., None]
    emission = jnp.where(source_column == target_column + phonon_shift, phonon_weight[0], 0.0)
    absorption = jnp.where(source_column == target_column - phonon_shift, phonon_weight[1], 0.0)
    return jnp.sum(emission + absorption, axis=-1)


def body(green_ret, prev_lesser, coupling_index, coupling_values, phonon_shift, phonon_weight):
    green = green_ret[0, 0]
    coupling = dense_coupling(coupling_index[0], coupling_values[0])
    coupling_t = coupling.T
    lead, tail = slice(0, BW), slice(SLAB_ORBITALS - BW, SLAB_ORBITALS)
    g_ll, g_rl, g_lr = green[:, lead, lead], green[:, tail, lead], green[:, lead, tail]

    energy = lax.axis_index("energy")
    flipped = energy + 2 - 4 * (energy // 2 % 2)
    sources = jnp.stack([energy, energy ^ 1, flipped, flipped ^ 1]).astype(jnp.int32)
    targets = (energy + 4 * jnp.arange(4, dtype=jnp.int32)) % 16
    weights = partner_weights(targets[:, None], sources[None, :], phonon_shift, phonon_weight).reshape(16)

    sigma, transfer, inward, corner, retarded, reach = phonon(
        weights, prev_lesser[0, 0], g_rl, g_lr, g_ll, coupling, coupling_t
    )
    outer_right, outer_rr, outer_rl, outer_left, outer_blocks = local_terms(green, sigma)
    lesser_far, retarded_part, lesser_part = sweep(
        green, transfer, inward, corner, retarded, reach, coupling, coupling_t, g_ll, g_rl,
        outer_rr, outer_rl, outer_left, outer_right, outer_blocks,
    )
    retarded, lesser = final_terms(green, lesser_far, retarded_part, lesser_part)
    return retarded[None, None], lesser[None, None]


def solution(mesh):
    placed = (
        P("slab", "energy", None, None, None),
        P("slab", "energy", None, None, None),
        P("slab", None, None),
        P("slab", None, None, None),
        P(),
        P(),
    )
    return jax.shard_map(
        body,
        mesh=mesh,
        in_specs=placed,
        out_specs=(P("slab", "energy", None, None, None), P("slab", "energy", None, None, None)),
        check_vma=False,
    )
```

time: 221 us -> 198 us (0.90)
  Pallas kernels: 210 us -> 189 us
  local copies, waits for them, and re-layouts: 7.39 us -> 5.14 us
    pallas_call x3, Pallas kernels: 189 us -> 167 us  [the longest x1 92.3 us: phonon(): pl.pallas_call(phonon_kernel, out_shape=[shape((2, SLAB_ORBITALS, BLK), b...]
    squeeze x1 -> x0, local copies, waits for them, and re-layouts: 2.25 us -> none  [body(): outer_right[0]]
where the time goes in v3:
time: 198 us
  Pallas kernels  189 us (95%)
  local copies, waits for them, and re-layouts  5.14 us (3%)
    pallas_call x1, Pallas kernels, phonon(): pl.pallas_call(phonon_kernel, out_shape=[shape((2, SLAB_ORBITALS, BLK), b...  92.3 us
    pallas_call x1, Pallas kernels, sweep(): pl.pallas_call(sweep_kernel, out_shape=[shape(WIDE, bf16)] + [shape((2, S...  67.8 us
    pallas_call x1, Pallas kernels, local_terms(): pl.pallas_call(local_kernel, out_shape=[shape((PAIRS, 2, BW, BW)), shape(...  22.1 us
    pallas_call x1, Pallas kernels, final_terms(): pl.pallas_call(final_kernel, grid=(PAIRS,), out_shape=[shape((2, SLAB_ORB...  6.91 us

profile of v3, /device:TPU:0, one launch (start us, length us, event | category | flops | bytes accessed | tf_op | source)
XLA Modules:
  0.0 197.7 jit_solution(10341614951267047489)
XLA Ops:
  0.7 0.1 pad_add_fusion
  0.8 0.8 slice_bitcast_fusion.1
  1.5 0.8 slice_bitcast_fusion.3
  2.3 0.7 broadcast_add_fusion
  3.0 0.1 add_reduce_fusion
  3.1 0.6 reshape.79.weights
  3.7 1.7 convolution_bitcast_fusion
  5.4 0.2 copy.13
  5.6 0.0 copy-start
  5.6 0.8 copy.14.coupling
  6.5 2.0 %fusion.8 = (bf16[2,256,256]{2,1,0:T(8,128)(2,1)}, bf16[2,256,256]{2,1,0:T(8,128)(2,1)}, bf16[2,256,256]{2,1,0:T(8,128)(2,1)}) fusion(bf16[2,1536,1536]{2,1,0:T(8,128)(2,1)} %bitcast.40), kind=kLoop, calls=%fused_computation.23 | loop fusion | bytes 1572864 | tf_op jit(solution)/shard_map/slice | solution.py:760
  8.5 0.0 copy-done
  8.5 92.3 %shard_map.77 = (bf16[2,1536,128]{2,1,0:T(8,128)(2,1)}, f32[4,256,512]{2,1,0:T(8,128)}, f32[4,256,512]{2,1,0:T(8,128)}, f32[4,256,512]{2,1,0:T(8,128)}, f32[256,512]{1,0:T(8,128)}, /*index=5*/f32[256,512]{1,0:T(8,128)}) custom-call(f32[16]{0:T(128)} %reshape.79.weights, f32[2,1536,128]{2,1,0:T(8,128)} %bitcast.47, ...), custom_call_target="tpu_custom_call" | custom-call | tf_op jit(solution)/shard_map/pallas_call | solution.py:643
  100.8 22.1 %shard_map.78 = (f32[6,2,256,256]{3,2,1,0:T(8,128)}, f32[2,256,256]{2,1,0:T(8,128)}, f32[2,256,256]{2,1,0:T(8,128)}, f32[2,256,256]{2,1,0:T(8,128)}, f32[2,1536,128]{2,1,0:T(8,128)}) custom-call(bf16[2,1536,1536]{2,1,0:T(8,128)(2,1)} %bitcast.41, bf16[2,1536,128]{2,1,0:T(8,128)(2,1)} %get-tuple-element.23.sigma), custom_call_target="tpu_custom_call" | custom-call | tf_op jit(solution)/shard_map/pallas_call | solution.py:704
  122.9 67.8 %shard_map.79 = (bf16[256,512]{1,0:T(8,128)(2,1)}, f32[2,1536,128]{2,1,0:T(8,128)}, f32[2,1536,128]{2,1,0:T(8,128)}) custom-call(f32[4,256,512]{2,1,0:T(8,128)} %get-tuple-element.18.transfer, f32[4,256,512]{2,1,0:T(8,128)} %get-tuple-element.19.inward, f32[4,256,512]{2,1,0:T(8,128)} %get-tuple-element.20.corner, f32[256,512]{1,0:T(8,128)} %get-tuple-element.21.retarded, ...), custom_call_target="tpu_custom_call" | custom-call | tf_op jit(solution)/shard_map/pallas_call | solution.py:674
  190.8 6.9 %shard_map.80 = (f32[2,1536,128]{2,1,0:T(8,128)}, f32[2,1536,128]{2,1,0:T(8,128)}) custom-call(bf16[2,1536,1536]{2,1,0:T(8,128)(2,1)} %bitcast.43, bf16[256,512]{1,0:T(8,128)(2,1)} %get-tuple-element.29.lesser_far, f32[2,1536,128]{2,1,0:T(8,128)} %get-tuple-element.30.retarded_part, f32[2,1536,128]{2,1,0:T(8,128)} %get-tuple-element.31.lesser_part), custom_call_target="tpu_custom_call" | custom-call | tf_op jit(solution)/shard_map/pallas_call | solution.py:722
  (3 shorter events, 0.0 us)
Async XLA Ops:
  5.6 2.9 %copy-start = (f32[32,8,2,128]{3,1,2,0:T(8,128)}, f32[32,8,2,128]{3,1,2,0:T(8,128)S(1)}, u32[]{:S(2)}) copy-start(f32[32,8,2,128]{3,1,2,0:T(8,128)S(1)} %copy.25) | copy-start | bytes 786436

commit v4 on v3

v4 whole, which is shorter than its diff:
```python
import functools

import jax
import jax.numpy as jnp
from jax import lax
from jax.experimental import pallas as pl
from jax.experimental.pallas import tpu as pltpu
from jax.sharding import PartitionSpec as P

SLAB_ORBITALS = 1536
BW = 256
BLK = 128
NBLK = 12
NBW = 2
NMODE = 3
NNZ = 3
PAIRS = SLAB_ORBITALS // BW
HALF = 4

MESH = pl.DeviceIdType.MESH
VMEM_LIMIT = 61 * 1024 * 1024
NN = (((1,), (0,)), ((), ()))
NT = (((1,), (1,)), ((), ()))

f32 = jnp.float32
bf16 = jnp.bfloat16


def dot(left, right, dims=NN):
    return lax.dot_general(left, right, dims, preferred_element_type=f32)


def split(value):
    high = value.astype(bf16)
    return high, (value - high.astype(f32)).astype(bf16)


def turned(value):
    width = value.shape[1] // 2
    return jnp.concatenate([-value[:, width:], value[:, :width]], axis=1)


def doubled(value):
    return jnp.concatenate([value, turned(value)], axis=0)


def product(left, right, dims=NN):
    left_high, left_low = split(left)
    right_high, right_low = split(right)
    main = doubled(right_high)
    return (
        dot(left_high, main, dims) + dot(left_low, main, dims) + dot(left_high, doubled(right_low), dims)
    )


def real_left(matrix, value):
    matrix_high, matrix_low = split(matrix)
    value_high, value_low = split(value)
    return dot(matrix_high, value_high) + dot(matrix_high, value_low) + dot(matrix_low, value_high)


def real_right(value, matrix):
    matrix_high, matrix_low = split(matrix)
    parts = []
    for part in (value[:, :BW], value[:, BW:]):
        high, low = split(part)
        parts.append(dot(high, matrix_high) + dot(low, matrix_high) + dot(high, matrix_low))
    return jnp.concatenate(parts, axis=1)


def beside(ref):
    return jnp.concatenate([ref[0], ref[1]], axis=1)


def adjoint(value):
    return jnp.concatenate([value[:, :BW].T, -value[:, BW:].T], axis=1)


class Place:
    def __init__(self):
        slab, energy = lax.axis_index("slab"), lax.axis_index("energy")
        self.half = slab // HALF
        self.z = slab % HALF
        base = self.half * HALF
        self.right = {"slab": base + (self.z + 1) % HALF}
        self.left = {"slab": base + (self.z + HALF - 1) % HALF}
        self.away = [{"slab": base + (self.z + d) % HALF} for d in (1, 2, 3)]
        other_half = (slab + HALF) % (2 * HALF)
        flipped = energy + 2 - 4 * (energy // 2 % 2)
        self.across = {"slab": other_half}
        self.y_partner = {"energy": flipped}
        self.energy, self.flipped = energy, flipped
        self.core = {"energy": energy + 1 - 2 * (energy % 2)}
        self.x_next = {"energy": (energy + 4) % 16}
        self.x_before = {"energy": (energy + 12) % 16}


def enter(others):
    barrier = pltpu.get_barrier_semaphore()
    for other in others:
        pl.semaphore_signal(barrier, inc=1, device_id=other, device_id_type=MESH)
    pl.semaphore_wait(barrier, len(others))


def sending(source, target, send, recv, device):
    return pltpu.make_async_remote_copy(
        src_ref=source, dst_ref=target, send_sem=send, recv_sem=recv, device_id=device, device_id_type=MESH
    )


class Gather:
    def __init__(self, place, slots, send, recv):
        z = place.z
        low, high = pl.ds(0, BW // 2), pl.ds(BW // 2, BW // 2)
        before, after, opposite = (z + 3) % HALF, (z + 1) % HALF, (z + 2) % HALF

        def copy(index, slot, rows, target):
            part = slots.at[slot, rows]
            return sending(part, part, send.at[index], recv.at[index], target)

        self.first = [
            copy(0, z, low, place.right),
            copy(1, z, high, place.left),
            copy(2, z, high, place.right),
            copy(3, z, low, place.left),
        ]
        self.arrive = [
            copy(0, before, low, place.right),
            copy(1, after, high, place.left),
            copy(2, before, high, place.right),
            copy(3, after, low, place.left),
        ]
        self.relay = [copy(4, before, low, place.right), copy(5, after, high, place.left)]
        self.last = [copy(4, opposite, low, place.right), copy(5, opposite, high, place.left)]

    def start(self):
        for item in self.first:
            item.start()

    def forward(self):
        for index in (0, 1):
            self.arrive[index].wait_recv()
            self.relay[index].start()

    def finish(self):
        for item in self.arrive[2:] + self.last:
            item.wait_recv()
        for item in self.first + self.relay:
            item.wait_send()


CHUNKS = 6
ROWS = SLAB_ORBITALS // CHUNKS
QUARTER = BW // HALF
STRIPE = 512


def unit():
    row = lax.broadcasted_iota(jnp.int32, WIDE, 0)
    column = lax.broadcasted_iota(jnp.int32, WIDE, 1)
    return (row == column).astype(f32)


class Shipment:
    def __init__(self, place, term, parts, quarter, total, send, recv):
        z = place.z

        def rows(index):
            return pl.ds(pl.multiple_of((index % HALF) * QUARTER, QUARTER), QUARTER)

        self.term, self.parts, self.quarter, self.here = term, parts, quarter, rows(z)
        self.spread = [
            sending(term.at[rows(z + d)], parts.at[d - 1], send.at[d - 1], recv.at[d - 1], place.away[d - 1])
            for d in (1, 2, 3)
        ]
        self.cross = sending(quarter, total.at[rows(z)], send.at[3], recv.at[3], place.across)
        self.hand = [
            sending(total.at[rows(z)], total.at[rows(z)], send.at[3 + d], recv.at[3 + d], place.away[d - 1])
            for d in (1, 2, 3)
        ]
        self.get = [
            sending(total.at[rows(z - d)], total.at[rows(z - d)], send.at[3 + d], recv.at[3 + d], place.away[d - 1])
            for d in (1, 2, 3)
        ]

    def start(self):
        for item in self.spread:
            item.start()

    def pass_over(self):
        for item in self.spread:
            item.wait_recv()
        self.quarter[...] = self.term[self.here, :] + self.parts[0] + self.parts[1] + self.parts[2]
        self.cross.start()

    def hand_on(self):
        self.cross.wait_recv()
        for item in self.hand:
            item.start()

    def arrive(self):
        for item in self.get:
            item.wait_recv()

    def sent(self):
        for item in self.spread + [self.cross]:
            item.wait_send()

    def handed(self):
        for item in self.hand:
            item.wait_send()


def partner_weights(target, sources, shift, weight):
    result = []
    for source in sources:
        total = 0.0
        for mode in range(NMODE):
            total = total + jnp.where(source == target + shift[mode], weight[0, mode], 0.0)
            total = total + jnp.where(source == target - shift[mode], weight[1, mode], 0.0)
        result.append(total)
    return result


def dense_coupling(index, values, coupling, coupling_t):
    for row in range(NBW):
        for column in range(NBW):
            block = jnp.zeros((BLK, BLK), f32)
            for item in range(NNZ):
                here = (index[item, 0] == row) & (index[item, 1] == column)
                block = block + jnp.where(here, 1.0, 0.0) * values[item]
            rows, columns = pl.ds(row * BLK, BLK), pl.ds(column * BLK, BLK)
            coupling[rows, columns] = block
            coupling_t[columns, rows] = block.T


def sweep_kernel(
    shift, weight, index, values, previous, green_hbm,
    lesser_far, retarded_part, lesser_part,
    green, coupling, coupling_t, transfer, inward, corner,
    others, two_away, after, before, passing, from_before, from_after,
    scaled, outer_right, outer_left, source, driven, weighted,
    run, incoming, own, through, term, total, reach, near, parts, quarter,
    load, z_send, z_recv, y_send, y_recv, core_send, core_recv, x_send, x_recv,
    cross_send, cross_recv, ship_send, ship_recv,
):
    place = Place()
    z, half = place.z, place.half
    steps = range(CHUNKS)
    left, last = pl.ds(0, BW), pl.ds(SLAB_ORBITALS - BW, BW)
    middle = pl.ds(BW, SLAB_ORBITALS - 2 * BW)
    fetch = [
        pltpu.make_async_copy(green_hbm.at[:, span], green.at[:, span], load.at[i])
        for i, span in enumerate((last, left, middle))
    ]
    for item in fetch:
        item.start()
    enter(place.away + [place.across, place.y_partner, place.core, place.x_next, place.x_before])


    def rows(c):
        return pl.ds(c * ROWS, ROWS)

    def part(ref, i):
        return lambda c: ref.at[i, rows(c)]

    def both(ref):
        return lambda c: ref.at[:, rows(c)]

    def copies(sems, kind, origin, target, device):
        send, recv = sems
        return [sending(origin(c), target(c), send.at[kind, c], recv.at[kind, c], device) for c in steps]

    y, core, x = (y_send, y_recv), (core_send, core_recv), (x_send, x_recv)
    over_y = copies(y, 0, both(previous), both(others.at[1]), place.y_partner)
    core_own = copies(core, 0, both(previous), both(others.at[0]), place.core)
    core_more = copies(core, 1, both(others.at[1]), both(others.at[2]), place.core)
    two_low = copies(x, 0, part(two_away, 0), part(passing, 0), place.x_next)
    two_high = copies(x, 1, part(two_away, 1), part(passing, 1), place.x_before)
    after_high = copies(x, 2, part(after, 1), part(from_before, 1), place.x_next)
    before_low = copies(x, 3, part(before, 0), part(from_after, 0), place.x_before)
    after_low = copies(x, 4, part(after, 0), part(from_before, 0), place.x_next)
    before_high = copies(x, 5, part(before, 1), part(from_after, 1), place.x_before)

    for c in (0, 1):
        over_y[c].start()
    for c in steps:
        core_own[c].start()

    sources = [place.energy, place.energy + 1 - 2 * (place.energy % 2)]
    sources += [place.flipped, place.flipped + 1 - 2 * (place.flipped % 2)]
    weights = [partner_weights((place.energy + 4 * t) % 16, sources, shift, weight) for t in range(4)]
    dense_coupling(index, values, coupling, coupling_t)
    turn = [Gather(place, ref, z_send.at[i], z_recv.at[i]) for i, ref in enumerate((transfer, inward, corner))]

    def near_factors():
        t_high, t_low = split(coupling_t[...])
        fetch[0].wait()
        value = jnp.concatenate([green[0, last, left], green[1, last, left]], axis=1)
        transfer[z] = dot(t_high, value) + dot(t_low, value)
        turn[0].start()
        fetch[1].wait()
        c_high, c_low = split(coupling[...])
        halves = [dot(green[i, left, last], c_high) + dot(green[i, left, last], c_low) for i in (0, 1)]
        inward[z] = jnp.concatenate(halves, axis=1)
        corner[z] = jnp.concatenate([green[0, left, left], green[1, left, left]], axis=1).astype(f32)
        fetch[2].wait()

    def weigh(c):
        over_y[c].wait_recv()
        core_more[c].start()
        if c + 2 < CHUNKS:
            over_y[c + 2].start()
        core_own[c].wait_recv()
        core_more[c].wait_recv()
        pieces = [previous[:, rows(c)]] + [others[i, :, rows(c)] for i in (0, 1, 2)]

        def sums(target):
            result = weights[target][0] * pieces[0]
            for i in (1, 2, 3):
                result = result + weights[target][i] * pieces[i]
            return result

        two_away[:, rows(c)] = sums(2)
        two_low[c].start()
        two_high[c].start()
        after[:, rows(c)] = sums(1)
        after_high[c].start()
        before[:, rows(c)] = sums(3)
        before_low[c].start()

    def add_passing(c):
        two_low[c].wait_recv()
        after[0, rows(c)] = after[0, rows(c)] + passing[0, rows(c)]
        after_low[c].start()
        two_high[c].wait_recv()
        before[1, rows(c)] = before[1, rows(c)] + passing[1, rows(c)]
        before_high[c].start()

    def self_energy(c):
        mine = weights[0][0] * previous[:, rows(c)]
        for i in (0, 1, 2):
            mine = mine + weights[0][i + 1] * others[i, :, rows(c)]
        for item in (after_high, before_low, after_low, before_high):
            item[c].wait_recv()
        return (mine + from_before[:, rows(c)] + from_after[:, rows(c)]).astype(bf16)


    def against(values, left_rows, right_rows, columns):
        first = values[0:2, left_rows, :].reshape(2 * BW, BW)
        second = values[1:3, left_rows, :].reshape(2 * BW, BW)
        result = dot(first, green[0, right_rows, columns], NT) + dot(second, green[1, right_rows, columns], NT)
        return result.reshape(2, BW, BW)

    def keep(span, result):
        scaled[0, span[0], span[1]] = result[:, : result.shape[1] // 2]
        scaled[1, span[0], span[1]] = result[:, result.shape[1] // 2 :]
        scaled[2, span[0], span[1]] = -result[:, : result.shape[1] // 2]

    def local_terms(c):
        sigma = self_energy(c)
        for k in (0, 1):
            real, imag = sigma[0, k * BLK : (k + 1) * BLK], sigma[1, k * BLK : (k + 1) * BLK]
            factor = doubled(jnp.concatenate([real, imag], axis=1))
            columns = pl.ds(c * BW + k * BLK, BLK)
            for start in range(0, SLAB_ORBITALS, STRIPE):
                span = pl.ds(start, STRIPE)
                piece = jnp.concatenate([green[0, span, columns], green[1, span, columns]], axis=1)
                keep((span, pl.ds(k * BLK, BLK)), dot(piece, factor).astype(bf16))
        columns = pl.ds(c * BW, BW)

        def pair(m, _):
            span = pl.ds(pl.multiple_of(m * BW, BW), BW)
            far = against(scaled, last, span, columns)
            outer_right[m] = far if c == 0 else outer_right[m] + far
            local = against(scaled, span, span, columns)
            for k in (0, 1):
                block = pl.ds(pl.multiple_of(m * BW + k * BLK, BLK), BLK)
                here = slice(k * BLK, (k + 1) * BLK)
                value = local[:, here, here]
                lesser_part[:, block, :] = value if c == 0 else lesser_part[:, block, :] + value

            @pl.when(m == 0)
            def _():
                outer_left[...] = local if c == 0 else outer_left[...] + local

            return 0

        lax.fori_loop(0, PAIRS, pair, 0)

    def reaches():
        reach[...] = unit()
        near[...] = unit()

        def over_transfer(ref):
            def step(j, _):
                ref[...] = product(transfer[j], ref[...])
                return 0

            return step

        def over_inward(ref):
            def step(i, _):
                j = HALF - 1 - i
                ref[...] = product(inward[j], ref[...])
                return 0

            return step

        @pl.when(half == 0)
        def _():
            lax.fori_loop(z + 1, HALF, over_transfer(reach), 0)
            lax.fori_loop(0, HALF - 1 - z, over_inward(near), 0)

        @pl.when(half == 1)
        def _():
            lax.fori_loop(HALF - z, HALF, over_inward(reach), 0)
            lax.fori_loop(0, z, over_transfer(near), 0)

    for t in range(CHUNKS + 2):
        if t < CHUNKS:
            weigh(t)
        if t == 0:
            near_factors()
        if t in (1, 3, 5):
            turn[t // 2].forward()
            if t < 5:
                turn[t // 2 + 1].start()
        if 0 <= t - 1 < CHUNKS:
            add_passing(t - 1)
        if t == CHUNKS:
            turn[0].finish()
            turn[1].finish()
            reaches()
        if 0 <= t - 2 < CHUNKS:
            local_terms(t - 2)


    ship = Shipment(place, term, parts, quarter, total, ship_send, ship_recv)
    over = sending(run, incoming, cross_send, cross_recv, place.across)

    def congruence(factor, value):
        return product(product(factor, value), factor, NT)

    gather = Gather(place, source, z_send.at[3], z_recv.at[3])
    source[z] = real_left(coupling_t[...], real_right(beside(outer_right.at[PAIRS - 1]), coupling[...]))

    @pl.when(half == 0)
    def _():
        term[...] = congruence(reach[...], source[z])
        ship.start()

    gather.start()

    @pl.when(half == 0)
    def _():
        ship.pass_over()

    gather.forward()
    turn[2].finish()

    def retarded_step(i, _):
        j = HALF - 1 - i

        @pl.when(j == z)
        def _():
            own[...] = run[...]

        run[...] = corner[j] + product(product(inward[j], run[...]), transfer[j])
        return 0

    @pl.when(half == 1)
    def _():
        own[...] = jnp.zeros_like(own)
        run[...] = corner[HALF - 1]
        lax.fori_loop(1, HALF, retarded_step, 0)
        over.start()

    @pl.when(half == 0)
    def _():
        over.wait_recv()
        run[...] = incoming[...]
        lax.fori_loop(0, HALF - 1 - z, retarded_step, 0)
        own[...] = run[...]

    def use_retarded():
        outer = real_right(own[...], coupling_t[...])
        through[...] = product(inward[z], outer)
        factor = doubled(real_left(coupling[...], outer).astype(bf16))
        for start in range(0, SLAB_ORBITALS, STRIPE):
            span = pl.ds(start, STRIPE)
            piece = jnp.concatenate([green[0, span, last], green[1, span, last]], axis=1)
            weighted[span, :] = dot(piece, factor).astype(bf16)

        def pair(m, _):
            span = pl.ds(pl.multiple_of(m * BW, BW), BW)
            result = dot(
                weighted[span, :], doubled(jnp.concatenate([green[0, last, span], green[1, last, span]], axis=1))
            )
            for k in (0, 1):
                block = pl.ds(pl.multiple_of(m * BW + k * BLK, BLK), BLK)
                here = slice(k * BLK, (k + 1) * BLK)
                for i in (0, 1):
                    there = slice(i * BW + k * BLK, i * BW + (k + 1) * BLK)
                    retarded_part[i, block, :] = green[i, block, block].astype(f32) + result[here, there]
            return 0

        lax.fori_loop(0, PAIRS, pair, 0)

    use_retarded()

    @pl.when(half == 1)
    def _():
        ship.hand_on()

    gather.finish()
    own[...] = jnp.zeros_like(own)

    def forward_step(j, _):
        own[...] = congruence(transfer[j], own[...]) + source[j]
        return 0

    @pl.when(z > 0)
    def _():
        own[...] = source[0]

    lax.fori_loop(1, z, forward_step, 0)

    @pl.when(half == 1)
    def _():
        ship.arrive()
        own[...] = own[...] + congruence(near[...], total[...])

    state = doubled(own[...].astype(bf16))
    corner_l = jnp.concatenate([green[0, left, left], green[1, left, left]], axis=1)
    corner_rl = jnp.concatenate([green[0, last, left], green[1, last, left]], axis=1)
    edge = dot(jnp.concatenate([corner_l, corner_rl], axis=0), state).astype(bf16)
    right = dot(edge, doubled(corner_l), NT)
    mixed = product(through[...], beside(outer_right.at[0]) + right[BW:])
    gather = Gather(place, driven, z_send.at[4], z_recv.at[4])
    driven[z] = beside(outer_left) + right[:BW] + mixed + adjoint(mixed)

    @pl.when(half == 1)
    def _():
        term[...] = congruence(reach[...], driven[z])
        ship.start()

    gather.start()

    @pl.when(half == 1)
    def _():
        ship.pass_over()

    gather.forward()

    for start in range(0, SLAB_ORBITALS, STRIPE):
        span = pl.ds(start, STRIPE)
        piece = jnp.concatenate([green[0, span, left], green[1, span, left]], axis=1)
        keep((span, pl.ds(0, BW)), dot(piece, state).astype(bf16))

    def pair(m, _):
        span = pl.ds(pl.multiple_of(m * BW, BW), BW)
        far_right = (outer_right[m] + against(scaled, last, span, left)).astype(bf16)
        mixed = dot(weighted[span, :], doubled(jnp.concatenate([far_right[0], far_right[1]], axis=1)))
        local = against(scaled, span, span, left)
        for k in (0, 1):
            block = pl.ds(pl.multiple_of(m * BW + k * BLK, BLK), BLK)
            here = slice(k * BLK, (k + 1) * BLK)
            for i in (0, 1):
                there = slice(i * BW + k * BLK, i * BW + (k + 1) * BLK)
                mix = mixed[here, there]
                mirrored = mix.T if i == 0 else -mix.T
                lesser_part[i, block, :] = lesser_part[i, block, :] + local[i, here, here] + mix + mirrored
        return 0

    lax.fori_loop(0, PAIRS, pair, 0)

    @pl.when(half == 0)
    def _():
        ship.hand_on()

    gather.finish()
    own[...] = jnp.zeros_like(own)

    def backward_step(i, _):
        j = HALF - 1 - i
        own[...] = congruence(inward[j], own[...]) + driven[j]
        return 0

    @pl.when(z < HALF - 1)
    def _():
        own[...] = driven[HALF - 1]

    lax.fori_loop(1, HALF - 1 - z, backward_step, 0)

    @pl.when(half == 0)
    def _():
        ship.arrive()
        own[...] = own[...] + congruence(near[...], total[...])

    lesser_far[...] = real_left(coupling[...], real_right(own[...], coupling_t[...])).astype(bf16)
    ship.sent()
    ship.handed()

    @pl.when(half == 1)
    def _():
        over.wait_send()

    for group in (
        over_y, core_own, core_more, two_low, two_high, after_high, before_low, after_low, before_high,
    ):
        for item in group:
            item.wait_send()


def final_kernel(green, lesser_far, retarded_part, lesser_part, retarded_out, lesser_out):
    right = jnp.concatenate([green[0], green[1]], axis=1)
    weighted = dot(right, doubled(lesser_far[...])).astype(bf16)
    real, imag = weighted[:, :BW], weighted[:, BW:]
    first = jnp.concatenate([real, imag], axis=0)
    second = jnp.concatenate([imag, -real], axis=0)
    total = dot(first, green[0], NT) + dot(second, green[1], NT)
    retarded_out[...] = retarded_part[...]
    for k in (0, 1):
        block = slice(k * BLK, (k + 1) * BLK)
        for i in (0, 1):
            here = slice(i * BW + k * BLK, i * BW + (k + 1) * BLK)
            lesser_out[i, block, :] = lesser_part[i, block, :] + total[here, block]


def whole(count):
    return [pl.BlockSpec(memory_space=pltpu.VMEM)] * count


def shape(dims, dtype=f32):
    return jax.ShapeDtypeStruct(dims, dtype)


WIDE = (BW, 2 * BW)


def sweep(shift, weight, index, values, previous, green):
    def wide(count):
        return [pltpu.VMEM(WIDE, f32)] * count

    def stacked(count):
        return [pltpu.VMEM((2, SLAB_ORBITALS, BLK), f32)] * count

    def slots(count):
        return [pltpu.VMEM((HALF,) + WIDE, f32)] * count

    dma = pltpu.SemaphoreType.DMA
    return pl.pallas_call(
        sweep_kernel,
        out_shape=[shape(WIDE, bf16)] + [shape((2, SLAB_ORBITALS, BLK))] * 2,
        in_specs=[pl.BlockSpec(memory_space=pltpu.SMEM)] * 3 + whole(2) + [pl.BlockSpec(memory_space=pl.ANY)],
        out_specs=whole(3),
        scratch_shapes=[pltpu.VMEM((2, SLAB_ORBITALS, SLAB_ORBITALS), bf16)]
        + [pltpu.VMEM((BW, BW), f32)] * 2
        + slots(3)
        + [pltpu.VMEM((3, 2, SLAB_ORBITALS, BLK), f32)]
        + stacked(6)
        + [
            pltpu.VMEM((3, SLAB_ORBITALS, BW), bf16),
            pltpu.VMEM((PAIRS, 2, BW, BW), f32),
            pltpu.VMEM((2, BW, BW), f32),
        ]
        + slots(2)
        + [pltpu.VMEM((SLAB_ORBITALS, 2 * BW), bf16)]
        + wide(8)
        + [pltpu.VMEM((3, QUARTER, 2 * BW), f32), pltpu.VMEM((QUARTER, 2 * BW), f32)]
        + [dma((3,)), dma((5, 6)), dma((5, 6))]
        + [dma((1, CHUNKS)), dma((1, CHUNKS)), dma((2, CHUNKS)), dma((2, CHUNKS)), dma((6, CHUNKS)), dma((6, CHUNKS))]
        + [dma, dma, dma((7,)), dma((7,))],
        compiler_params=pltpu.CompilerParams(
            collective_id=0, has_side_effects=True, vmem_limit_bytes=VMEM_LIMIT
        ),
    )(shift, weight, index, values, previous, green)


def final_terms(*operands):
    strip = pl.BlockSpec((2, BW, BLK), lambda m: (0, m, 0))
    return pl.pallas_call(
        final_kernel,
        grid=(PAIRS,),
        out_shape=[shape((2, SLAB_ORBITALS, BLK))] * 2,
        in_specs=[
            pl.BlockSpec((2, BW, BW), lambda m: (0, m, PAIRS - 1)),
            pl.BlockSpec(WIDE, lambda m: (0, 0)),
            strip,
            strip,
        ],
        out_specs=[strip, strip],
        compiler_params=pltpu.CompilerParams(vmem_limit_bytes=VMEM_LIMIT),
    )(*operands)


def body(green_ret, prev_lesser, coupling_index, coupling_values, phonon_shift, phonon_weight):
    green = green_ret[0, 0]
    lesser_far, retarded_part, lesser_part = sweep(
        phonon_shift, phonon_weight, coupling_index[0], coupling_values[0], prev_lesser[0, 0], green
    )
    retarded, lesser = final_terms(green, lesser_far, retarded_part, lesser_part)
    return retarded[None, None], lesser[None, None]


def solution(mesh):
    placed = (
        P("slab", "energy", None, None, None),
        P("slab", "energy", None, None, None),
        P("slab", None, None),
        P("slab", None, None, None),
        P(),
        P(),
    )
    return jax.shard_map(
        body,
        mesh=mesh,
        in_specs=placed,
        out_specs=(P("slab", "energy", None, None, None), P("slab", "energy", None, None, None)),
        check_vma=False,
    )
```

time: 198 us -> 145 us (0.73)
  Pallas kernels: 189 us -> 143 us
  local copies, waits for them, and re-layouts: 5.14 us -> 1.34 us
    pallas_call x2 -> x0, Pallas kernels: 114 us -> none  [the longest x1 92.3 us: phonon(): pl.pallas_call(phonon_kernel, out_shape=[shape((2, SLAB_ORBITALS, BLK), b...]
    pallas_call x1, Pallas kernels: 67.8 us -> 136 us  [sweep(): pl.pallas_call(sweep_kernel, out_shape=[shape(WIDE, bf16)] + [shape((2, S...]
    slice x1 -> x0, local copies, waits for them, and re-layouts: 2 us -> none  [body(): green[:, lead, lead]]
where the time goes in v4:
time: 145 us
  Pallas kernels  143 us (99%)
    pallas_call x1, Pallas kernels, sweep(): pl.pallas_call(sweep_kernel, out_shape=[shape(WIDE, bf16)] + [shape((2, S...  136 us
    pallas_call x1, Pallas kernels, final_terms(): pl.pallas_call(final_kernel, grid=(PAIRS,), out_shape=[shape((2, SLAB_ORB...  6.92 us

profile of v4, /device:TPU:0, one launch (start us, length us, event | category | flops | bytes accessed | tf_op | source)
XLA Modules:
  0.0 145.0 jit_solution(5406885033613755723)
XLA Ops:
  0.6 1.3 copy.8.index
  2.0 136.1 %shard_map.77 = (bf16[256,512]{1,0:T(8,128)(2,1)}, f32[2,1536,128]{2,1,0:T(8,128)}, f32[2,1536,128]{2,1,0:T(8,128)}) custom-call(s32[3]{0:T(128)} %shift.1, f32[2,3]{1,0:T(2,128)} %weight.1, s32[3,2]{1,0:T(4,128)} %copy.8.index, f32[3,128,128]{2,1,0:T(8,128)} %bitcast.9, f32[2,1536,128]{2,1,0:T(8,128)} %bitcast.8, bf16[2,1536,1536]{2,1,0:T(8,128)(2,1)} %bitcast.6), custom_call_target="tpu_custom_call" | custom-call | tf_op jit(solution)/shard_map/pallas_call | solution.py:653
  138.1 6.9 %shard_map.78 = (f32[2,1536,128]{2,1,0:T(8,128)}, f32[2,1536,128]{2,1,0:T(8,128)}) custom-call(bf16[2,1536,1536]{2,1,0:T(8,128)(2,1)} %bitcast.7, bf16[256,512]{1,0:T(8,128)(2,1)} %get-tuple-element.7.lesser_far, f32[2,1536,128]{2,1,0:T(8,128)} %get-tuple-element.8.retarded_part, f32[2,1536,128]{2,1,0:T(8,128)} %get-tuple-element.9.lesser_part), custom_call_target="tpu_custom_call" | custom-call | tf_op jit(solution)/shard_map/pallas_call | solution.py:683

commit v5 on v4

--- a/solution.py
+++ b/solution.py
@@ -149,7 +149,10 @@
             item.wait_send()
 
 
-CHUNKS = 6
+CHUNKS = 12
+ADD_LAG = 2
+USE_LAG = 4
+PIECES = 2
 ROWS = SLAB_ORBITALS // CHUNKS
 QUARTER = BW // HALF
 STRIPE = 512
@@ -164,50 +167,63 @@
 class Shipment:
     def __init__(self, place, term, parts, quarter, total, send, recv):
         z = place.z
-
-        def rows(index):
-            return pl.ds(pl.multiple_of((index % HALF) * QUARTER, QUARTER), QUARTER)
-
-        self.term, self.parts, self.quarter, self.here = term, parts, quarter, rows(z)
+        size = QUARTER // PIECES
+        pieces = range(PIECES)
+
+        def rows(index, piece):
+            return pl.ds(pl.multiple_of((index % HALF) * QUARTER + piece * size, size), size)
+
+        def within(piece):
+            return pl.ds(piece * size, size)
+
+        def copy(index, piece, origin, target, device):
+            return sending(origin, target, send.at[index, piece], recv.at[index, piece], device)
+
+        def handed(d, piece, index):
+            spot = total.at[rows(index, piece)]
+            return copy(3 + d, piece, spot, spot, place.away[d - 1])
+
+        self.term, self.parts, self.quarter = term, parts, quarter
+        self.here = [rows(z, p) for p in pieces]
+        self.within = [within(p) for p in pieces]
         self.spread = [
-            sending(term.at[rows(z + d)], parts.at[d - 1], send.at[d - 1], recv.at[d - 1], place.away[d - 1])
-            for d in (1, 2, 3)
+            [copy(d - 1, p, term.at[rows(z + d, p)], parts.at[d - 1, within(p)], place.away[d - 1]) for d in (1, 2, 3)]
+            for p in pieces
         ]
-        self.cross = sending(quarter, total.at[rows(z)], send.at[3], recv.at[3], place.across)
-        self.hand = [
-            sending(total.at[rows(z)], total.at[rows(z)], send.at[3 + d], recv.at[3 + d], place.away[d - 1])
-            for d in (1, 2, 3)
-        ]
-        self.get = [
-            sending(total.at[rows(z - d)], total.at[rows(z - d)], send.at[3 + d], recv.at[3 + d], place.away[d - 1])
-            for d in (1, 2, 3)
-        ]
+        self.cross = [copy(3, p, quarter.at[within(p)], total.at[rows(z, p)], place.across) for p in pieces]
+        self.hand = [[handed(d, p, z) for d in (1, 2, 3)] for p in pieces]
+        self.get = [[handed(d, p, z - d) for d in (1, 2, 3)] for p in pieces]
 
     def start(self):
-        for item in self.spread:
-            item.start()
+        for group in self.spread:
+            for item in group:
+                item.start()
 
     def pass_over(self):
-        for item in self.spread:
-            item.wait_recv()
-        self.quarter[...] = self.term[self.here, :] + self.parts[0] + self.parts[1] + self.parts[2]
-        self.cross.start()
+        for group, here, within, cross in zip(self.spread, self.here, self.within, self.cross):
+            for item in group:
+                item.wait_recv()
+            others = self.parts[0, within, :] + self.parts[1, within, :] + self.parts[2, within, :]
+            self.quarter[within, :] = self.term[here, :] + others
+            cross.start()
 
     def hand_on(self):
-        self.cross.wait_recv()
-        for item in self.hand:
-            item.start()
+        for cross, group in zip(self.cross, self.hand):
+            cross.wait_recv()
+            for item in group:
+                item.start()
 
     def arrive(self):
-        for item in self.get:
-            item.wait_recv()
+        for group in self.get:
+            for item in group:
+                item.wait_recv()
 
     def sent(self):
-        for item in self.spread + [self.cross]:
+        for item in sum(self.spread, self.cross):
             item.wait_send()
 
     def handed(self):
-        for item in self.hand:
+        for item in sum(self.hand, []):
             item.wait_send()
 
 
@@ -227,7 +243,7 @@
         for column in range(NBW):
             block = jnp.zeros((BLK, BLK), f32)
             for item in range(NNZ):
-                here = (index[item, 0] == row) & (index[item, 1] == column)
+                here = (index[0, item, 0] == row) & (index[0, item, 1] == column)
                 block = block + jnp.where(here, 1.0, 0.0) * values[item]
             rows, columns = pl.ds(row * BLK, BLK), pl.ds(column * BLK, BLK)
             coupling[rows, columns] = block
@@ -240,7 +256,7 @@
     green, coupling, coupling_t, transfer, inward, corner,
     others, two_away, after, before, passing, from_before, from_after,
     scaled, outer_right, outer_left, source, driven, weighted,
-    run, incoming, own, through, term, total, reach, near, parts, quarter,
+    run, incoming, own, through, term, total, reach, near, parts, quarter, weighting,
     load, z_send, z_recv, y_send, y_recv, core_send, core_recv, x_send, x_recv,
     cross_send, cross_recv, ship_send, ship_recv,
 ):
@@ -282,15 +298,15 @@
     after_low = copies(x, 4, part(after, 0), part(from_before, 0), place.x_next)
     before_high = copies(x, 5, part(before, 1), part(from_after, 1), place.x_before)
 
-    for c in (0, 1):
-        over_y[c].start()
-    for c in steps:
-        core_own[c].start()
+    over_y[0].start()
+    core_own[0].start()
 
     sources = [place.energy, place.energy + 1 - 2 * (place.energy % 2)]
     sources += [place.flipped, place.flipped + 1 - 2 * (place.flipped % 2)]
     weights = [partner_weights((place.energy + 4 * t) % 16, sources, shift, weight) for t in range(4)]
     dense_coupling(index, values, coupling, coupling_t)
+    over_y[1].start()
+    core_own[1].start()
     turn = [Gather(place, ref, z_send.at[i], z_recv.at[i]) for i, ref in enumerate((transfer, inward, corner))]
 
     def near_factors():
@@ -304,13 +320,13 @@
         halves = [dot(green[i, left, last], c_high) + dot(green[i, left, last], c_low) for i in (0, 1)]
         inward[z] = jnp.concatenate(halves, axis=1)
         corner[z] = jnp.concatenate([green[0, left, left], green[1, left, left]], axis=1).astype(f32)
-        fetch[2].wait()
 
     def weigh(c):
         over_y[c].wait_recv()
         core_more[c].start()
         if c + 2 < CHUNKS:
             over_y[c + 2].start()
+            core_own[c + 2].start()
         core_own[c].wait_recv()
         core_more[c].wait_recv()
         pieces = [previous[:, rows(c)]] + [others[i, :, rows(c)] for i in (0, 1, 2)]
@@ -357,22 +373,30 @@
         scaled[1, span[0], span[1]] = result[:, result.shape[1] // 2 :]
         scaled[2, span[0], span[1]] = -result[:, : result.shape[1] // 2]
 
+    def scale(c):
+        sigma = self_energy(c)
+        factor = doubled(jnp.concatenate([sigma[0], sigma[1]], axis=1))
+        columns = pl.ds(c * BLK, BLK)
+        for start in range(0, SLAB_ORBITALS, STRIPE):
+            span = pl.ds(start, STRIPE)
+            piece = jnp.concatenate([green[0, span, columns], green[1, span, columns]], axis=1)
+            keep((span, pl.ds(c % 2 * BLK, BLK)), dot(piece, factor).astype(bf16))
+
+    def last_pair(c):
+        far = against(scaled, last, last, pl.ds(c * BW, BW))
+        outer_right[PAIRS - 1] = far if c == 0 else outer_right[PAIRS - 1] + far
+
     def local_terms(c):
-        sigma = self_energy(c)
-        for k in (0, 1):
-            real, imag = sigma[0, k * BLK : (k + 1) * BLK], sigma[1, k * BLK : (k + 1) * BLK]
-            factor = doubled(jnp.concatenate([real, imag], axis=1))
-            columns = pl.ds(c * BW + k * BLK, BLK)
-            for start in range(0, SLAB_ORBITALS, STRIPE):
-                span = pl.ds(start, STRIPE)
-                piece = jnp.concatenate([green[0, span, columns], green[1, span, columns]], axis=1)
-                keep((span, pl.ds(k * BLK, BLK)), dot(piece, factor).astype(bf16))
         columns = pl.ds(c * BW, BW)
 
         def pair(m, _):
             span = pl.ds(pl.multiple_of(m * BW, BW), BW)
-            far = against(scaled, last, span, columns)
-            outer_right[m] = far if c == 0 else outer_right[m] + far
+
+            @pl.when(m < PAIRS - 1)
+            def _():
+                far = against(scaled, last, span, columns)
+                outer_right[m] = far if c == 0 else outer_right[m] + far
+
             local = against(scaled, span, span, columns)
             for k in (0, 1):
                 block = pl.ds(pl.multiple_of(m * BW + k * BLK, BLK), BLK)
@@ -417,23 +441,29 @@
             lax.fori_loop(HALF - z, HALF, over_inward(reach), 0)
             lax.fori_loop(0, z, over_transfer(near), 0)
 
-    for t in range(CHUNKS + 2):
+    near_factors()
+    for t in range(CHUNKS + USE_LAG):
         if t < CHUNKS:
             weigh(t)
-        if t == 0:
-            near_factors()
-        if t in (1, 3, 5):
-            turn[t // 2].forward()
-            if t < 5:
-                turn[t // 2 + 1].start()
-        if 0 <= t - 1 < CHUNKS:
-            add_passing(t - 1)
-        if t == CHUNKS:
+        if t == USE_LAG:
+            fetch[2].wait()
+        if t in (2, 6, 10):
+            i = (2, 6, 10).index(t)
+            turn[i].forward()
+            if i < 2:
+                turn[i + 1].start()
+        if 0 <= t - ADD_LAG < CHUNKS:
+            add_passing(t - ADD_LAG)
+        if t == CHUNKS + 0:
             turn[0].finish()
             turn[1].finish()
             reaches()
-        if 0 <= t - 2 < CHUNKS:
-            local_terms(t - 2)
+        if t >= USE_LAG:
+            scale(t - USE_LAG)
+            if (t - USE_LAG) % 2 == 1:
+                last_pair((t - USE_LAG) // 2)
+                if t < CHUNKS + USE_LAG - 1:
+                    local_terms((t - USE_LAG) // 2)
 
 
     ship = Shipment(place, term, parts, quarter, total, ship_send, ship_recv)
@@ -451,12 +481,6 @@
         ship.start()
 
     gather.start()
-
-    @pl.when(half == 0)
-    def _():
-        ship.pass_over()
-
-    gather.forward()
     turn[2].finish()
 
     def retarded_step(i, _):
@@ -476,6 +500,14 @@
         lax.fori_loop(1, HALF, retarded_step, 0)
         over.start()
 
+    local_terms(PAIRS - 1)
+
+    @pl.when(half == 0)
+    def _():
+        ship.pass_over()
+
+    gather.forward()
+
     @pl.when(half == 0)
     def _():
         over.wait_recv()
@@ -483,10 +515,12 @@
         lax.fori_loop(0, HALF - 1 - z, retarded_step, 0)
         own[...] = run[...]
 
+    outer = real_right(own[...], coupling_t[...])
+    through[...] = product(inward[z], outer)
+    weighting[...] = real_left(coupling[...], outer).astype(bf16)
+
     def use_retarded():
-        outer = real_right(own[...], coupling_t[...])
-        through[...] = product(inward[z], outer)
-        factor = doubled(real_left(coupling[...], outer).astype(bf16))
+        factor = doubled(weighting[...])
         for start in range(0, SLAB_ORBITALS, STRIPE):
             span = pl.ds(start, STRIPE)
             piece = jnp.concatenate([green[0, span, last], green[1, span, last]], axis=1)
@@ -507,10 +541,9 @@
 
         lax.fori_loop(0, PAIRS, pair, 0)
 
-    use_retarded()
-
     @pl.when(half == 1)
     def _():
+        use_retarded()
         ship.hand_on()
 
     gather.finish()
@@ -540,18 +573,22 @@
     gather = Gather(place, driven, z_send.at[4], z_recv.at[4])
     driven[z] = beside(outer_left) + right[:BW] + mixed + adjoint(mixed)
 
+    gather.start()
+
     @pl.when(half == 1)
     def _():
         term[...] = congruence(reach[...], driven[z])
         ship.start()
 
-    gather.start()
+    gather.forward()
 
     @pl.when(half == 1)
     def _():
         ship.pass_over()
 
-    gather.forward()
+    @pl.when(half == 0)
+    def _():
+        use_retarded()
 
     for start in range(0, SLAB_ORBITALS, STRIPE):
         span = pl.ds(start, STRIPE)
@@ -614,18 +651,22 @@
 
 
 def final_kernel(green, lesser_far, retarded_part, lesser_part, retarded_out, lesser_out):
-    right = jnp.concatenate([green[0], green[1]], axis=1)
-    weighted = dot(right, doubled(lesser_far[...])).astype(bf16)
-    real, imag = weighted[:, :BW], weighted[:, BW:]
-    first = jnp.concatenate([real, imag], axis=0)
-    second = jnp.concatenate([imag, -real], axis=0)
-    total = dot(first, green[0], NT) + dot(second, green[1], NT)
+    factor = doubled(lesser_far[...])
     retarded_out[...] = retarded_part[...]
-    for k in (0, 1):
-        block = slice(k * BLK, (k + 1) * BLK)
-        for i in (0, 1):
-            here = slice(i * BW + k * BLK, i * BW + (k + 1) * BLK)
-            lesser_out[i, block, :] = lesser_part[i, block, :] + total[here, block]
+    for start in range(0, STRIPE, BW):
+        span = slice(start, start + BW)
+        right = jnp.concatenate([green[0, span], green[1, span]], axis=1)
+        weighted = dot(right, factor).astype(bf16)
+        real, imag = weighted[:, :BW], weighted[:, BW:]
+        first = jnp.concatenate([real, imag], axis=0)
+        second = jnp.concatenate([imag, -real], axis=0)
+        total = dot(first, green[0, span], NT) + dot(second, green[1, span], NT)
+        for k in (0, 1):
+            block = slice(k * BLK, (k + 1) * BLK)
+            rows = slice(start + k * BLK, start + (k + 1) * BLK)
+            for i in (0, 1):
+                here = slice(i * BW + k * BLK, i * BW + (k + 1) * BLK)
+                lesser_out[i, rows, :] = lesser_part[i, rows, :] + total[here, block]
 
 
 def whole(count):
@@ -668,10 +709,10 @@
         + slots(2)
         + [pltpu.VMEM((SLAB_ORBITALS, 2 * BW), bf16)]
         + wide(8)
-        + [pltpu.VMEM((3, QUARTER, 2 * BW), f32), pltpu.VMEM((QUARTER, 2 * BW), f32)]
+        + [pltpu.VMEM((3, QUARTER, 2 * BW), f32), pltpu.VMEM((QUARTER, 2 * BW), f32), pltpu.VMEM(WIDE, bf16)]
         + [dma((3,)), dma((5, 6)), dma((5, 6))]
         + [dma((1, CHUNKS)), dma((1, CHUNKS)), dma((2, CHUNKS)), dma((2, CHUNKS)), dma((6, CHUNKS)), dma((6, CHUNKS))]
-        + [dma, dma, dma((7,)), dma((7,))],
+        + [dma, dma, dma((7, PIECES)), dma((7, PIECES))],
         compiler_params=pltpu.CompilerParams(
             collective_id=0, has_side_effects=True, vmem_limit_bytes=VMEM_LIMIT
         ),
@@ -679,13 +720,13 @@
 
 
 def final_terms(*operands):
-    strip = pl.BlockSpec((2, BW, BLK), lambda m: (0, m, 0))
+    strip = pl.BlockSpec((2, STRIPE, BLK), lambda m: (0, m, 0))
     return pl.pallas_call(
         final_kernel,
-        grid=(PAIRS,),
+        grid=(SLAB_ORBITALS // STRIPE,),
         out_shape=[shape((2, SLAB_ORBITALS, BLK))] * 2,
         in_specs=[
-            pl.BlockSpec((2, BW, BW), lambda m: (0, m, PAIRS - 1)),
+            pl.BlockSpec((2, STRIPE, BW), lambda m: (0, m, PAIRS - 1)),
             pl.BlockSpec(WIDE, lambda m: (0, 0)),
             strip,
             strip,
@@ -698,7 +739,7 @@
 def body(green_ret, prev_lesser, coupling_index, coupling_values, phonon_shift, phonon_weight):
     green = green_ret[0, 0]
     lesser_far, retarded_part, lesser_part = sweep(
-        phonon_shift, phonon_weight, coupling_index[0], coupling_values[0], prev_lesser[0, 0], green
+        phonon_shift, phonon_weight, coupling_index, coupling_values[0], prev_lesser[0, 0], green
     )
     retarded, lesser = final_terms(green, lesser_far, retarded_part, lesser_part)
     return retarded[None, None], lesser[None, None]

time: 145 us -> 143 us (0.986)
  Pallas kernels: 143 us -> 141 us
where the time goes in v5:
time: 143 us
  Pallas kernels  141 us (99%)
    pallas_call x1, Pallas kernels, sweep(): pl.pallas_call(sweep_kernel, out_shape=[shape(WIDE, bf16)] + [shape((2, S...  135 us
    pallas_call x1, Pallas kernels, final_terms(): pl.pallas_call(final_kernel, grid=(SLAB_ORBITALS // STRIPE,), out_shape=[...  5.97 us

profile of v5, /device:TPU:0, one launch (start us, length us, event | category | flops | bytes accessed | tf_op | source)
XLA Modules:
  0.0 142.7 jit_solution(975982608844764747)
XLA Ops:
  0.6 1.3 copy.8.index
  2.0 134.8 %shard_map.77 = (bf16[256,512]{1,0:T(8,128)(2,1)}, f32[2,1536,128]{2,1,0:T(8,128)}, f32[2,1536,128]{2,1,0:T(8,128)}) custom-call(s32[3]{0:T(128)} %shift.1, f32[2,3]{1,0:T(2,128)} %weight.1, s32[1,3,2]{2,1,0:T(4,128)} %copy.8.index, f32[3,128,128]{2,1,0:T(8,128)} %bitcast.8, f32[2,1536,128]{2,1,0:T(8,128)} %bitcast.7, bf16[2,1536,1536]{2,1,0:T(8,128)(2,1)} %bitcast.5), custom_call_target="tpu_custom_call" | custom-call | tf_op jit(solution)/shard_map/pallas_call | solution.py:694
  136.8 6.0 %shard_map.78 = (f32[2,1536,128]{2,1,0:T(8,128)}, f32[2,1536,128]{2,1,0:T(8,128)}) custom-call(bf16[2,1536,1536]{2,1,0:T(8,128)(2,1)} %bitcast.6, bf16[256,512]{1,0:T(8,128)(2,1)} %get-tuple-element.7.lesser_far, f32[2,1536,128]{2,1,0:T(8,128)} %get-tuple-element.8.retarded_part, f32[2,1536,128]{2,1,0:T(8,128)} %get-tuple-element.9.lesser_part), custom_call_target="tpu_custom_call" | custom-call | tf_op jit(solution)/shard_map/pallas_call | solution.py:724

commit v6 on v5

--- a/solution.py
+++ b/solution.py
@@ -243,7 +243,7 @@
         for column in range(NBW):
             block = jnp.zeros((BLK, BLK), f32)
             for item in range(NNZ):
-                here = (index[0, item, 0] == row) & (index[0, item, 1] == column)
+                here = (index[0, 0, item] == row) & (index[0, 1, item] == column)
                 block = block + jnp.where(here, 1.0, 0.0) * values[item]
             rows, columns = pl.ds(row * BLK, BLK), pl.ds(column * BLK, BLK)
             coupling[rows, columns] = block
@@ -739,7 +739,7 @@
 def body(green_ret, prev_lesser, coupling_index, coupling_values, phonon_shift, phonon_weight):
     green = green_ret[0, 0]
     lesser_far, retarded_part, lesser_part = sweep(
-        phonon_shift, phonon_weight, coupling_index, coupling_values[0], prev_lesser[0, 0], green
+        phonon_shift, phonon_weight, jnp.swapaxes(coupling_index, 1, 2), coupling_values[0], prev_lesser[0, 0], green
     )
     retarded, lesser = final_terms(green, lesser_far, retarded_part, lesser_part)
     return retarded[None, None], lesser[None, None]

time: 143 us -> 142 us (level)
  no operation moved by 1% of the time
where the time goes in v6:
time: 142 us; the launch traced here: 141 us
  Pallas kernels  141 us (99%)
    pallas_call x1, Pallas kernels, sweep(): pl.pallas_call(sweep_kernel, out_shape=[shape(WIDE, bf16)] + [shape((2, S...  135 us
    pallas_call x1, Pallas kernels, final_terms(): pl.pallas_call(final_kernel, grid=(SLAB_ORBITALS // STRIPE,), out_shape=[...  5.97 us

profile of v6, /device:TPU:0, one launch (start us, length us, event | category | flops | bytes accessed | tf_op | source)
XLA Modules:
  0.0 141.5 jit_solution(2307783619390637736)
XLA Ops:
  0.6 134.9 %shard_map.77 = (bf16[256,512]{1,0:T(8,128)(2,1)}, f32[2,1536,128]{2,1,0:T(8,128)}, f32[2,1536,128]{2,1,0:T(8,128)}) custom-call(s32[3]{0:T(128)} %shift.1, f32[2,3]{1,0:T(2,128)} %weight.1, s32[1,2,3]{2,1,0:T(2,128)} %bitcast.10, f32[3,128,128]{2,1,0:T(8,128)} %bitcast.9, f32[2,1536,128]{2,1,0:T(8,128)} %bitcast.8, bf16[2,1536,1536]{2,1,0:T(8,128)(2,1)} %bitcast.6), custom_call_target="tpu_custom_call" | custom-call | tf_op jit(solution)/shard_map/pallas_call | solution.py:694
  135.5 6.0 %shard_map.78 = (f32[2,1536,128]{2,1,0:T(8,128)}, f32[2,1536,128]{2,1,0:T(8,128)}) custom-call(bf16[2,1536,1536]{2,1,0:T(8,128)(2,1)} %bitcast.7, bf16[256,512]{1,0:T(8,128)(2,1)} %get-tuple-element.7.lesser_far, f32[2,1536,128]{2,1,0:T(8,128)} %get-tuple-element.8.retarded_part, f32[2,1536,128]{2,1,0:T(8,128)} %get-tuple-element.9.lesser_part), custom_call_target="tpu_custom_call" | custom-call | tf_op jit(solution)/shard_map/pallas_call | solution.py:724
